TPU v7x, 32 devices: a whole 2x2x4 slice. The times are simulated.
32 devices in a mesh: freq: 4 (over x, core), mode: 8 (over z, y).
Axes of the slice: x: 2, y: 2, z: 4, core: 2. Of those that a mesh axis runs over, the one named last changes fastest.
Arguments:
- mode_shapes: bfloat16 [6144, 3072], P(None, 'mode'), may hold values from -0.15625 to 0.15625
- modal_freq: float32 [3072], P('mode'), may hold values from 0.5 to 4
- damping: float32 [3072], P('mode'), may hold values from 0.05 to 0.2
- excitation: float32 [16], P('freq'), parts along dimension 0, may hold values from 0.5 to 4
- modal_load: float32 [3072, 16, 2, 64], P('mode', 'freq'), parts along dimension 1, may hold values from -6 to 6
- attach: int32 [8, 96], replicated, may hold values from 0 to 6143
- row_count: int32 [8], P('mode'), may hold values from 48 to 384, as said below
- otm: bfloat16 [8, 384, 96], P('mode'), may hold values from -0.625 to 0.625
Outputs:
- csd: bfloat16 [8, 16, 2, 384, 384], P('mode', 'freq'), parts along dimension 1
- joint_csd: bfloat16 [8, 16, 2, 128, 384], P('mode', 'freq'), parts along dimension 1
There are 4 independent parts, one for each index of `freq`. A program takes and returns all parts, laid end to end along the dimension named above; an argument that names none is the same for every part. Nothing has to cross between parts.
Inputs may be any that keep to these rules, and one draw needn't show every extreme that they name: `row_count`: at least one component has exactly 384 rows in every draw.
All inputs are finite; a program needn't handle non-finite values.
Results may differ from a plain program's by a relative error of at most 0.008.
Values may be sent and summed in bfloat16 or wider, within the bound.
No kernel may reach another device: no remote copies, remote signals or barrier semaphores. Data moves between devices by JAX's collectives and lax.ppermute only.
A program may use at most 128 MiB of HBM per device.

v0:
```python
import jax
import jax.numpy as jnp
from jax import lax
from jax.sharding import PartitionSpec as P

CROSS = 128


def shifted(value, axis, steps):
    count = lax.axis_size(axis)
    initial, last = (max(0, -steps), min(count, count - steps))
    return lax.ppermute(value, axis, [(source, source + steps) for source in range(initial, last)])


def per_device(mode_shapes, modal_freq, damping, excitation, modal_load, attach, row_count, otm):
    comp_here = otm.shape[0]
    rows_max = otm.shape[1]
    att_len = otm.shape[2]
    lines = excitation.shape[0]
    width = modal_load.shape[3]
    columns = lines * 2 * width
    omega_sq = modal_freq * modal_freq
    real_part = omega_sq[:, None] - (excitation * excitation)[None, :]
    imag_part = 2.0 * damping[:, None] * modal_freq[:, None] * excitation[None, :]
    denom = real_part * real_part + imag_part * imag_part
    frf_re = (omega_sq[:, None] * real_part / denom)[:, :, None]
    frf_im = (-omega_sq[:, None] * imag_part / denom)[:, :, None]
    load_re = modal_load[:, :, 0, :]
    load_im = modal_load[:, :, 1, :]
    resp_re = frf_re * load_re - frf_im * load_im
    resp_im = frf_re * load_im + frf_im * load_re
    modal_resp = jnp.stack([resp_re, resp_im], axis=2).astype(jnp.bfloat16)
    modal_resp = modal_resp.reshape(modal_resp.shape[0], columns)
    flat_attach = attach.reshape(-1)
    own_start = lax.axis_index("mode") * (comp_here * att_len)
    band = lax.psum_scatter(
        jnp.dot(mode_shapes, modal_resp, preferred_element_type=jnp.float32),
        "mode",
        scatter_dimension=0,
        tiled=True,
    ).astype(jnp.bfloat16)
    whole = lax.all_gather(band, "mode", axis=0, tiled=True)
    index_rows = lax.dynamic_slice_in_dim(flat_attach, own_start, comp_here * att_len)
    picked = jnp.take(whole, index_rows, axis=0)
    picked = picked.reshape(comp_here, att_len, columns)
    row_mask = jnp.arange(rows_max, dtype=jnp.int32)[None, :] < row_count[:, None]
    masked_otm = jnp.where(row_mask[:, :, None], otm, jnp.zeros_like(otm))
    factor = jnp.einsum(
        "cra,caj->crj", masked_otm, picked, preferred_element_type=jnp.float32
    ).astype(jnp.bfloat16)
    zmat = factor.reshape(comp_here, rows_max, lines, 2 * width)
    wmat = jnp.concatenate([zmat[..., width:], -zmat[..., :width]], axis=-1)
    following = shifted(zmat[0], "mode", -1)
    partner = jnp.concatenate([zmat[1:], following[None]], axis=0)
    block = 128
    z_here = zmat[0]
    w_here = wmat[0]
    needed = (row_count[0] + block - 1) // block

    def block_step(step, buffer):
        z_rows = lax.dynamic_slice_in_dim(z_here, step * block, block, 0)
        w_rows = lax.dynamic_slice_in_dim(w_here, step * block, block, 0)
        part_re = (
            jnp.einsum("rfk,sfk->frs", z_rows, z_here, preferred_element_type=jnp.float32) / width
        )
        part_im = (
            jnp.einsum("rfk,sfk->frs", w_rows, z_here, preferred_element_type=jnp.float32) / width
        )
        value = jnp.stack([part_re, part_im], axis=1).astype(jnp.bfloat16)
        zero = jnp.zeros((), jnp.int32)
        return lax.dynamic_update_slice(
            buffer, value, (zero, zero, (step * block).astype(jnp.int32), zero)
        )

    empty = jnp.zeros((lines, 2, rows_max, rows_max), jnp.bfloat16)
    auto_blocks = [lax.fori_loop(0, needed, block_step, empty)]
    csd = jnp.stack(auto_blocks, axis=0)
    joint_re = (
        jnp.einsum("crfk,csfk->cfrs", zmat[:, :CROSS], partner, preferred_element_type=jnp.float32)
        / width
    )
    joint_im = (
        jnp.einsum("crfk,csfk->cfrs", wmat[:, :CROSS], partner, preferred_element_type=jnp.float32)
        / width
    )
    joint_csd = jnp.stack([joint_re, joint_im], axis=2).astype(jnp.bfloat16)
    return (csd, joint_csd)


def solution(mesh):
    return jax.shard_map(
        per_device,
        mesh=mesh,
        in_specs=(
            P(None, "mode"),
            P("mode"),
            P("mode"),
            P("freq"),
            P("mode", "freq", None, None),
            P(),
            P("mode"),
            P("mode", None, None),
        ),
        out_specs=(P("mode", "freq", None, None, None), P("mode", "freq", None, None, None)),
        check_vma=False,
    )
```

profile of v0, /device:TPU:0, one launch (start us, length us, event | category | flops | bytes accessed | tf_op | source)
XLA Modules:
  0.0 365.7 jit_solution(12492316789184048241)
XLA Ops:
  7.2 0.0 reduce-scatter.2.cloned.1.call-start
  7.2 0.7 mul.124
  7.9 0.7 multiply_multiply_fusion.2
  8.6 0.7 fusion.22
  9.4 1.2 subtract_convert_fusion
  10.7 8.8 %convolution_bitcast_fusion = f32[6144,512]{0,1:T(8,128)} fusion(bf16[384,512]{0,1:T(8,128)(2,1)S(1)} %bitcast.54, bf16[6144,384]{1,0:T(8,128)(2,1)} %param.10), kind=kOutput, calls=%fused_computation.13 | convolution fusion | flops 2415919104 | bytes 17694720 | tf_op jit(solution)/shard_map/dot_general | solution.py:37
  19.5 0.0 all-gather.2.cloned.1.call-start
  19.5 210.1 %reduce-scatter.2.cloned.1.call-done = f32[768,512]{0,1:T(8,128)} async-done(((f32[6144,512]{0,1:T(8,128)}), f32[768,512]{0,1:T(8,128)}) %reduce-scatter.2.cloned.1.call-update) | async-done | bytes 1572880 | tf_op jit(solution)/shard_map/reduce_scatter | solution.py:36
  229.6 2.4 convert_element_type.23
  232.7 0.1 reshape.261
  232.8 0.1 compare_and_fusion
  232.9 97.7 %all-gather.2.cloned.1.call-done = bf16[6144,512]{0,1:T(8,128)(2,1)} async-done(((bf16[768,512]{0,1:T(8,128)(2,1)}), bf16[6144,512]{0,1:T(8,128)(2,1)}) %all-gather.2.cloned.1.call-update) | async-done | bytes 6291472 | tf_op jit(solution)/shard_map/all_gather | solution.py:42
  330.6 8.6 %copy.10 = bf16[6144,512]{1,0:T(8,128)(2,1)} copy(bf16[6144,512]{0,1:T(8,128)(2,1)} %all-gather.2.cloned.1.call-done) | data formatting | bytes 12582912 | tf_op jit(solution)/shard_map/all_gather | solution.py:42
  339.2 4.4 %gather_fusion = bf16[96,512]{1,0:T(8,128)(2,1)S(1)} fusion(bf16[6144,512]{1,0:T(8,128)(2,1)} %copy.10, s32[1024]{0:T(1024)S(1)} %pad_clamp_fusion), kind=kCustom, calls=%fused_computation | custom fusion | bytes 196992 | tf_op jit(solution)/shard_map/jit(_take)/gather | solution.py:44
  343.6 0.3 convolution_convert_fusion
  344.0 0.1 reshape.262
  344.1 0.8 copy_bitcast_fusion
  344.9 0.4 fusion.28
  345.2 0.1 copy.20
  345.3 0.1 copy_negate_fusion
  345.4 1.3 collective-permute-start
  346.7 0.2 maximum_bitcast_fusion
  346.9 1.6 broadcast_in_dim.21.clone
  348.5 3.7 %while.10 = (s32[]{:T(128)}, bf16[4,2,384,384]{3,2,1,0:T(8,128)(2,1)}, s32[]{:T(128)}, bf16[384,4,128]{2,0,1:T(8,128)(2,1)}, bf16[384,4,128]{2,0,1:T(8,128)(2,1)...) while((s32[]{:T(128)}, bf16[4,2,384,384]{3,2,1,0:T(8,128)(2,1)}, s32[]{:T(128)}, ...), condition=%wide.region_2.3_spmd, body=%wide.region_1.2_spmd.sunk | while | flops 101842944 | bytes 3408023 | solution.py:76
  348.5 1.3 fusion.46
  349.8 1.4 fusion.47
  351.2 1.0 copy_dynamic-update-slice_fusion.2
  352.2 4.9 %collective-permute-done = bf16[384,4,128]{2,0,1:T(8,128)(2,1)S(1)} collective-permute-done((bf16[384,4,128]{2,0,1:T(8,128)(2,1)}, bf16[384,4,128]{2,0,1:T(8,128)(2,1)S(1)}, u32[]{:S(2)}, u32[]{:S(2)}) %collective-permute-start) | collective-permute-done | bytes 393248 | tf_op jit(solution)/shard_map/ppermute | solution.py:12
  357.2 0.3 fusion.10
  357.5 0.3 fusion.11
  357.8 0.1 pad_maximum_fusion.1
  357.9 1.0 copy.17
  (10 shorter events, 0.1 us)
Async XLA Ops:
  7.2 222.5 %reduce-scatter.2.cloned.1.call-start = ((), (), s32[]{:S(2)}) async-start(), calls=%async_computation.1 | async-start | bytes 14155776 | tf_op jit(solution)/shard_map/reduce_scatter | solution.py:36
  19.4 213.2 %copy-start.1 = (s32[8,96]{1,0:T(8,128)S(1)}, s32[8,96]{1,0:T(8,128)}, u32[]{:S(2)}) copy-start(s32[8,96]{1,0:T(8,128)} %param.15) | copy-start | bytes 9220
  19.5 311.1 %all-gather.2.cloned.1.call-start = ((), (), s32[]{:S(2)}) async-start(), calls=%async_computation.2 | async-start | bytes 7077888 | tf_op jit(solution)/shard_map/all_gather | solution.py:42
  232.9 110.8 %copy-start = (bf16[1,384,96]{1,2,0:T(8,128)(2,1)S(1)}, bf16[1,384,96]{1,2,0:T(8,128)(2,1)}, u32[]{:S(2)}) copy-start(bf16[1,384,96]{1,2,0:T(8,128)(2,1)} %param.17) | copy-start | bytes 221188
  345.4 11.8 %collective-permute-start = (bf16[384,4,128]{2,0,1:T(8,128)(2,1)}, bf16[384,4,128]{2,0,1:T(8,128)(2,1)S(1)}, u32[]{:S(2)}, u32[]{:S(2)}) collective-permute-start(bf16[384,4,128]{2,0,1:T(8,128)(2,1)} %copy_bitcast_fusion), channel_id=1, source_target_pairs={{1,0},{2,1},{3,2},{4,3},{5,4},{6,5},{7,6},{9,8},{10,9},{11,10},{12... | collective-permute-start | bytes 1179656 | tf_op jit(solution)/shard_map/ppermute | solution.py:12
Sparse Core Ops, SparseCore 0:
  19.6 210.0 reduce-scatter.1
  232.4 98.1 all-gather.1
where the time goes:
time: 368 us; the launch traced here: 366 us
  waiting for transfers between devices  313 us (85%)
  local copies, waits for them, and re-layouts  17.1 us (5%)
  between operations  14.8 us (4%)
  matrix products  12.4 us (3%)
  other arithmetic  7.26 us (2%)
    reduce_scatter x1, waiting for transfers between devices, per_device(): lax.psum_scatter(jnp.dot(mode_shapes, modal_resp, preferred_element_type=...  210 us
    all_gather x1, waiting for transfers between devices, per_device(): whole = lax.all_gather(band, 'mode', axis=0, tiled=True)  97.7 us
    dot_general x1, matrix products, per_device(): jnp.dot(mode_shapes, modal_resp, preferred_element_type=jnp.float32)  8.78 us
    all_gather x1, local copies, waits for them, and re-layouts, per_device(): whole = lax.all_gather(band, 'mode', axis=0, tiled=True)  8.65 us
  transfers between devices with their start and end apart: 3, of which 3 were waited for; matrix products, arithmetic and copies ran while one was open for 2% of the time, Pallas kernels for 0%

commit v1 on v0

v1 whole, which is shorter than its diff:
```python
import functools

import jax
import jax.numpy as jnp
from jax import lax
from jax.experimental import pallas as pl
from jax.experimental.pallas import tpu as pltpu
from jax.sharding import PartitionSpec as P

CROSS = 128
CHUNKS = 12
F32 = jnp.float32
BF16 = jnp.bfloat16
NT = (((1,), (1,)), ((), ()))
TN = (((0,), (0,)), ((), ()))


def modal_response(freq_ref, damp_ref, exc_ref, load_ref, resp_ref):
    lines = load_ref.shape[0]
    width = load_ref.shape[2]
    freq = freq_ref[...]
    damp = damp_ref[...]
    omega_sq = freq * freq
    for f in range(lines):
        exc = exc_ref[f]
        a = omega_sq - exc * exc
        b = 2.0 * damp * freq * exc
        denom = a * a + b * b
        frf_re = omega_sq * a / denom
        frf_im = -omega_sq * b / denom
        load_re = load_ref[f, 0]
        load_im = load_ref[f, 1]
        base = f * 2 * width
        resp_ref[base : base + width, :] = (frf_re * load_re - frf_im * load_im).astype(BF16)
        resp_ref[base + width : base + 2 * width, :] = (
            frf_re * load_im + frf_im * load_re
        ).astype(BF16)


def fetch(shapes_ref, raw, wide, sems, start_only):
    count = sems.shape[0]
    step = raw.shape[0] // count

    def copy(i):
        rows = pl.ds(pl.multiple_of(i * step, step), step)
        return pltpu.make_async_copy(shapes_ref.at[rows, :], raw.at[rows, :], sems.at[i])

    if start_only:
        for i in range(count):
            copy(i).start()
        return

    def body(i, carry):
        copy(i).wait()
        rows = pl.ds(pl.multiple_of(i * step, step), step)
        wide[rows, :] = raw[rows, :].astype(F32)
        return carry

    lax.fori_loop(0, count, body, 0)


def product(attach_ref, wide, rows_ref, resp_ref, comp):
    count = rows_ref.shape[0]
    unroll = 16 if count % 16 == 0 else 1

    def body(b, carry):
        for u in range(unroll):
            a = b * unroll + u
            rows_ref[pl.ds(a, 1), :] = wide[pl.ds(attach_ref[comp, a], 1), :]
        return carry

    lax.fori_loop(0, count // unroll, body, 0)
    return lax.dot_general(
        rows_ref[...].astype(BF16), resp_ref[...], NT, preferred_element_type=F32
    )


def far_kernel(
    slots, attach_ref, exc_ref, freq_ref, damp_ref, load_hbm, shapes_ref, *rest
):
    outs = rest[: len(slots)]
    resp_ref, load_ref, raw, wide, rows_ref, sems, load_sem = rest[len(slots) :]
    load = pltpu.make_async_copy(load_hbm, load_ref, load_sem)
    load.start()
    fetch(shapes_ref, raw, wide, sems, True)
    me = lax.axis_index("mode")
    load.wait()
    modal_response(freq_ref, damp_ref, exc_ref, load_ref, resp_ref)
    fetch(shapes_ref, raw, wide, sems, False)
    for slot, out in zip(slots, outs):
        part = product(attach_ref, wide, rows_ref, resp_ref, jnp.bitwise_xor(me, slot))
        out[...] = part.astype(out.dtype)


def near_kernel(slots, attach_ref, resp_ref, shapes_ref, *rest):
    outs = rest[: len(slots)]
    raw, wide, rows_ref, sems = rest[len(slots) :]
    fetch(shapes_ref, raw, wide, sems, True)
    me = lax.axis_index("mode")
    fetch(shapes_ref, raw, wide, sems, False)
    for slot, out in zip(slots, outs):
        part = product(attach_ref, wide, rows_ref, resp_ref, jnp.bitwise_xor(me, slot))
        out[...] = part.astype(out.dtype)


def cross_block(left_re, left_im, right, scale):
    left = jnp.concatenate([left_re, left_im], axis=0)
    value = lax.dot_general(left, right, NT, preferred_element_type=F32) * scale
    return value.astype(BF16)


def turned(z):
    width = z.shape[1] // 2
    return jnp.concatenate([z[:, width:], -z[:, :width]], axis=1)


def auto_kernel(count_ref, otm_ref, picked_ref, csd_ref):
    rows_max = otm_ref.shape[1]
    pair = picked_ref.shape[1]
    z = lax.dot_general(otm_ref[...], picked_ref[...], TN, preferred_element_type=F32)
    keep = lax.broadcasted_iota(jnp.int32, z.shape, 0) < count_ref[0]
    z = jnp.where(keep, z, 0.0).astype(BF16)
    value = cross_block(z, turned(z), z, 2.0 / pair)
    csd_ref[0] = value[:rows_max]
    csd_ref[1] = value[rows_max:]


def joint_kernel(count_ref, otm_ref, picked_ref, next_otm_ref, next_picked_ref, joint_ref):
    cross = joint_ref.shape[1]
    pair = picked_ref.shape[1]
    z = lax.dot_general(
        otm_ref[:, :cross], picked_ref[...], TN, preferred_element_type=F32
    )
    keep = lax.broadcasted_iota(jnp.int32, z.shape, 0) < count_ref[0]
    z = jnp.where(keep, z, 0.0).astype(BF16)
    after = lax.dot_general(
        next_otm_ref[...], next_picked_ref[...], TN, preferred_element_type=F32
    ).astype(BF16)
    value = cross_block(z, turned(z), after, 2.0 / pair)
    joint_ref[0] = value[:cross]
    joint_ref[1] = value[cross:]


def per_device(mode_shapes, modal_freq, damping, excitation, modal_load, attach, row_count, otm):
    count = lax.axis_size("mode")
    half = count // 2
    iface, modes = mode_shapes.shape
    rows_max, att = otm.shape[1], otm.shape[2]
    lines = excitation.shape[0]
    width = modal_load.shape[3]
    pair = 2 * width
    columns = lines * pair
    smem = pl.BlockSpec(memory_space=pltpu.SMEM)
    vmem = pl.BlockSpec(memory_space=pltpu.VMEM)
    hbm = pl.BlockSpec(memory_space=pl.ANY)
    load_t = jnp.transpose(modal_load, (1, 2, 3, 0))
    otm_t = jnp.transpose(otm[0], (1, 0))
    part = jax.ShapeDtypeStruct((att, columns), BF16)
    part_wide = jax.ShapeDtypeStruct((att, columns), F32)
    chunks = CHUNKS if iface % (16 * CHUNKS) == 0 else 1
    scratch = [
        pltpu.VMEM((iface, modes), BF16),
        pltpu.VMEM((iface, modes), F32),
        pltpu.VMEM((att, modes), F32),
        pltpu.SemaphoreType.DMA((chunks,)),
    ]
    params = pltpu.CompilerParams(vmem_limit_bytes=40 << 20)
    steps = list(range(1, half))
    far_slots = [half ^ k for k in steps] + [half]
    near_slots = steps + [0]
    *far, far_own, resp = pl.pallas_call(
        functools.partial(far_kernel, far_slots),
        out_shape=[part] * (half - 1)
        + [part_wide, jax.ShapeDtypeStruct((columns, modes), BF16)],
        in_specs=[smem, smem, vmem, vmem, hbm, hbm],
        out_specs=[vmem] * (half + 1),
        scratch_shapes=[pltpu.VMEM(load_t.shape, F32)] + scratch + [pltpu.SemaphoreType.DMA],
        compiler_params=params,
        name="far_parts",
    )(attach, excitation, modal_freq.reshape(1, -1), damping.reshape(1, -1), load_t, mode_shapes)
    *near, near_own = pl.pallas_call(
        functools.partial(near_kernel, near_slots),
        out_shape=[part] * (half - 1) + [part_wide],
        in_specs=[smem, vmem, hbm],
        out_specs=[vmem] * half,
        scratch_shapes=scratch,
        compiler_params=params,
        name="near_parts",
    )(attach, resp, mode_shapes)

    def swapped(value, k):
        return lax.ppermute(value, "mode", [(i, i ^ k) for i in range(count)])

    def following(value):
        return lax.ppermute(value, "mode", [(i, i - 1) for i in range(1, count)])

    far_sum = far_own
    for k, value in zip(steps, far):
        far_sum = far_sum + swapped(value, k).astype(F32)
    picked = near_own
    for k, value in zip(steps, near):
        picked = picked + swapped(value, k).astype(F32)
    picked = picked + swapped(far_sum.astype(BF16), half).astype(F32)
    picked = picked.astype(BF16)

    keep = jnp.arange(rows_max, dtype=jnp.int32)[None, :] < row_count[:, None]
    next_otm = following(jnp.where(keep, otm_t, jnp.zeros_like(otm_t)))
    next_picked = following(picked)

    columns_of = pl.BlockSpec((att, pair), lambda f: (0, f))
    whole = pl.BlockSpec((att, rows_max), lambda f: (0, 0))
    csd = pl.pallas_call(
        auto_kernel,
        grid=(lines,),
        out_shape=jax.ShapeDtypeStruct((1, lines, 2, rows_max, rows_max), BF16),
        in_specs=[smem, whole, columns_of],
        out_specs=pl.BlockSpec((None, None, 2, rows_max, rows_max), lambda f: (0, f, 0, 0, 0)),
        name="auto_csd",
    )(row_count, otm_t, picked)
    joint = pl.pallas_call(
        joint_kernel,
        grid=(lines,),
        out_shape=jax.ShapeDtypeStruct((1, lines, 2, CROSS, rows_max), BF16),
        in_specs=[smem, whole, columns_of, whole, columns_of],
        out_specs=pl.BlockSpec((None, None, 2, CROSS, rows_max), lambda f: (0, f, 0, 0, 0)),
        name="joint_csd",
    )(row_count, otm_t, picked, next_otm, next_picked)
    return (csd, joint)


def solution(mesh):
    return jax.shard_map(
        per_device,
        mesh=mesh,
        in_specs=(
            P(None, "mode"),
            P("mode"),
            P("mode"),
            P("freq"),
            P("mode", "freq", None, None),
            P(),
            P("mode"),
            P("mode", None, None),
        ),
        out_specs=(P("mode", "freq", None, None, None), P("mode", "freq", None, None, None)),
        check_vma=False,
    )
```

time: 368 us -> 50.6 us (0.14)
  the two profiles are of different devices: /device:TPU:0 before, /device:TPU:16 now
where the time goes in v1:
time: 50.6 us; the launch traced here: 49.9 us
  Pallas kernels  21.2 us (42%)
  starting transfers between devices  14.1 us (28%)
  local copies, waits for them, and re-layouts  7.46 us (15%)
  waiting for transfers between devices  5.6 us (11%)
  between operations  1.39 us (3%)
    ppermute x7, starting transfers between devices, swapped(): return lax.ppermute(value, 'mode', [(i, i ^ k) for i in range(count)])  7.24 us
    ppermute x2, starting transfers between devices, following(): return lax.ppermute(value, 'mode', [(i, i - 1) for i in range(1, count)])  6.84 us
    pallas_call x1, Pallas kernels, per_device(): pl.pallas_call(functools.partial(far_kernel, far_slots), out_shape=[part]...  6.57 us
    pallas_call x1, Pallas kernels, per_device(): pl.pallas_call(functools.partial(near_kernel, near_slots), out_shape=[par...  6.39 us
    unnamed x18, local copies, waits for them, and re-layouts  6.09 us
    ppermute x7, waiting for transfers between devices, swapped(): return lax.ppermute(value, 'mode', [(i, i ^ k) for i in range(count)])  5.59 us
    pallas_call x1, Pallas kernels, per_device(): pl.pallas_call(auto_kernel, grid=(lines,), out_shape=jax.ShapeDtypeStruct...  4.35 us
    pallas_call x1, Pallas kernels, per_device(): pl.pallas_call(joint_kernel, grid=(lines,), out_shape=jax.ShapeDtypeStruc...  3.9 us
  transfers between devices with their start and end apart: 9, of which 4 were waited for; matrix products, arithmetic and copies ran while one was open for 0% of the time, Pallas kernels for 22%

profile of v1, /device:TPU:16, one launch (start us, length us, event | category | flops | bytes accessed | tf_op | source)
XLA Modules:
  0.0 49.9 jit_solution(795161599625646422)
XLA Ops:
  0.6 0.7 %reshape.18.freq_ref = f32[1,384]{1,0:T(1,128)S(1)} reshape(f32[384]{0:T(512)} %param.9) | data formatting | bytes 3072 | tf_op jit(solution)/shard_map/reshape | solution.py:180
  1.3 0.7 %reshape.19.damp_ref = f32[1,384]{1,0:T(1,128)S(1)} reshape(f32[384]{0:T(512)} %param.10) | data formatting | bytes 3072 | tf_op jit(solution)/shard_map/reshape | solution.py:180
  2.0 2.3 %copy-done = bf16[6144,384]{1,0:T(8,128)(2,1)S(1)} copy-done((bf16[6144,384]{1,0:T(8,128)(2,1)S(1)}, bf16[6144,384]{1,0:T(8,128)(2,1)}, u32[]{:S(2)}) %copy-start) | copy-done | bytes 4718616
  4.3 1.1 %copy-done.2 = f32[384,4,2,64]{0,3,2,1:T(8,128)S(1)} copy-done((f32[384,4,2,64]{0,3,2,1:T(8,128)S(1)}, f32[384,4,2,64]{0,3,2,1:T(8,128)}, u32[]{:S(2)}) %copy-start.2) | copy-done | bytes 786456
  5.5 0.7 %copy-done.3 = s32[8,96]{1,0:T(8,128)S(1)} copy-done((s32[8,96]{1,0:T(8,128)S(1)}, s32[8,96]{1,0:T(8,128)}, u32[]{:S(2)}) %copy-start.3) | copy-done | bytes 3096
  6.2 0.7 %copy-done.4 = f32[4]{0:T(128)S(1)} copy-done((f32[4]{0:T(128)S(1)}, f32[4]{0:T(128)}, u32[]{:S(2)}) %copy-start.4) | copy-done | bytes 40
  6.8 6.6 %far_parts.1 = (bf16[96,512]{1,0:T(8,128)(2,1)S(1)}, bf16[96,512]{1,0:T(8,128)(2,1)S(1)}, bf16[96,512]{1,0:T(8,128)(2,1)S(1)}, f32[96,512]{1,0:T(8,128)S(1)}, bf16[512,384]{1,0:T(8,128)(2,1)S(1)}) custom-call(s32[8,96]{1,0:T(8,128)S(1)} %copy-done.3, f32[4]{0:T(128)S(1)} %copy-done.4, f32[1,384]{1,0:T(1,128)S(1)} %reshape.18.freq_ref, ...), custom_call_target="tpu_custom_call" | custom-call | tf_op jit(solution)/shard_map/far_parts/pallas_call | solution.py:171
  13.4 1.6 %collective-permute-start.3 = (bf16[96,512]{1,0:T(8,128)(2,1)S(1)}, bf16[96,512]{1,0:T(8,128)(2,1)S(1)}, u32[]{:S(2)}, u32[]{:S(2)}) collective-permute-start(bf16[96,512]{1,0:T(8,128)(2,1)S(1)} %get-tuple-element.17), channel_id=1, source_target_pairs={{0,1},{1,0},{2,3},{3,2},{4,5},{5,4},{6,7},{7,6},{8,9},{9,8},{10,11... | collective-permute-start | bytes 294920 | tf_op jit(solution)/shard_map/ppermute | solution.py:192
  15.0 1.6 %collective-permute-start.4 = (bf16[96,512]{1,0:T(8,128)(2,1)S(1)}, bf16[96,512]{1,0:T(8,128)(2,1)S(1)}, u32[]{:S(2)}, u32[]{:S(2)}) collective-permute-start(bf16[96,512]{1,0:T(8,128)(2,1)S(1)} %get-tuple-element.18), channel_id=1, source_target_pairs={{0,2},{1,3},{2,0},{3,1},{4,6},{5,7},{6,4},{7,5},{8,10},{9,11},{10,... | collective-permute-start | bytes 294920 | tf_op jit(solution)/shard_map/ppermute | solution.py:192
  16.6 0.4 collective-permute-start.5
  17.0 6.4 %near_parts.1 = (bf16[96,512]{1,0:T(8,128)(2,1)S(1)}, bf16[96,512]{1,0:T(8,128)(2,1)S(1)}, bf16[96,512]{1,0:T(8,128)(2,1)S(1)}, f32[96,512]{1,0:T(8,128)S(1)}) custom-call(s32[8,96]{1,0:T(8,128)S(1)} %copy-done.3, bf16[512,384]{1,0:T(8,128)(2,1)S(1)} %get-tuple-element.11.resp_ref, bf16[6144,384]{1,0:T(8,128)(2,1)S(1)} %copy-done.1), custom_call_target="tpu_custom_call" | custom-call | tf_op jit(solution)/shard_map/near_parts/pallas_call | solution.py:181
  23.4 1.6 %collective-permute-start = (bf16[96,512]{1,0:T(8,128)(2,1)S(1)}, bf16[96,512]{1,0:T(8,128)(2,1)S(1)}, u32[]{:S(2)}, u32[]{:S(2)}) collective-permute-start(bf16[96,512]{1,0:T(8,128)(2,1)S(1)} %get-tuple-element.13), channel_id=1, source_target_pairs={{0,1},{1,0},{2,3},{3,2},{4,5},{5,4},{6,7},{7,6},{8,9},{9,8},{10,11... | collective-permute-start | bytes 294920 | tf_op jit(solution)/shard_map/ppermute | solution.py:192
  24.9 1.6 %collective-permute-start.1 = (bf16[96,512]{1,0:T(8,128)(2,1)S(1)}, bf16[96,512]{1,0:T(8,128)(2,1)S(1)}, u32[]{:S(2)}, u32[]{:S(2)}) collective-permute-start(bf16[96,512]{1,0:T(8,128)(2,1)S(1)} %get-tuple-element.14), channel_id=1, source_target_pairs={{0,2},{1,3},{2,0},{3,1},{4,6},{5,7},{6,4},{7,5},{8,10},{9,11},{10,... | collective-permute-start | bytes 294920 | tf_op jit(solution)/shard_map/ppermute | solution.py:192
  27.2 0.0 collective-permute-done.3
  27.2 0.5 collective-permute-start.2
  27.6 0.0 collective-permute-done.4
  27.6 0.0 collective-permute-done.5
  27.6 0.1 add_convert_fusion.1
  27.7 0.1 collective-permute-start.6
  27.8 0.2 collective-permute-done
  28.0 2.6 %collective-permute-done.1 = bf16[96,512]{1,0:T(8,128)(2,1)S(1)} collective-permute-done((bf16[96,512]{1,0:T(8,128)(2,1)S(1)}, bf16[96,512]{1,0:T(8,128)(2,1)S(1)}, u32[]{:S(2)}, u32[]{:S(2)}) %collective-permute-start.1) | collective-permute-done | bytes 98336 | tf_op jit(solution)/shard_map/ppermute | solution.py:192
  30.6 2.2 %collective-permute-done.2 = bf16[96,512]{1,0:T(8,128)(2,1)S(1)} collective-permute-done((bf16[96,512]{1,0:T(8,128)(2,1)S(1)}, bf16[96,512]{1,0:T(8,128)(2,1)S(1)}, u32[]{:S(2)}, u32[]{:S(2)}) %collective-permute-start.2) | collective-permute-done | bytes 98336 | tf_op jit(solution)/shard_map/ppermute | solution.py:192
  32.8 0.6 %collective-permute-done.6 = bf16[96,512]{1,0:T(8,128)(2,1)S(1)} collective-permute-done((bf16[96,512]{1,0:T(8,128)(2,1)S(1)}, bf16[96,512]{1,0:T(8,128)(2,1)S(1)}, u32[]{:S(2)}, u32[]{:S(2)}) %collective-permute-start.6) | collective-permute-done | bytes 98336 | tf_op jit(solution)/shard_map/ppermute | solution.py:192
  33.4 0.1 add_convert_fusion.picked_ref
  33.5 3.8 %collective-permute-start.8 = (bf16[96,512]{1,0:T(8,128)(2,1)S(1)}, bf16[96,512]{1,0:T(8,128)(2,1)S(1)}, u32[]{:S(2)}, u32[]{:S(2)}) collective-permute-start(bf16[96,512]{1,0:T(8,128)(2,1)S(1)} %add_convert_fusion.picked_ref), channel_id=1, source_target_pairs={{1,0},{2,1},{3,2},{4,3},{5,4},{6,5},{7,6},{9,8},{10,9},{11,10},{12... | collective-permute-start | bytes 294920 | tf_op jit(solution)/shard_map/ppermute | solution.py:195
  37.3 3.0 %collective-permute-start.7 = (bf16[96,384]{1,0:T(8,128)(2,1)S(1)}, bf16[96,384]{1,0:T(8,128)(2,1)S(1)}, u32[]{:S(2)}, u32[]{:S(2)}) collective-permute-start(bf16[96,384]{1,0:T(8,128)(2,1)S(1)} %broadcast_select_fusion), channel_id=1, source_target_pairs={{1,0},{2,1},{3,2},{4,3},{5,4},{6,5},{7,6},{9,8},{10,9},{11,10},{12... | collective-permute-start | bytes 221192 | tf_op jit(solution)/shard_map/ppermute | solution.py:195
  40.4 4.4 %auto_csd.1 = bf16[1,4,2,384,384]{4,3,2,1,0:T(8,128)(2,1)} custom-call(s32[1]{0:T(128)} %copy.10.count_ref, bf16[96,384]{1,0:T(8,128)(2,1)} %bitcast.8, bf16[96,512]{1,0:T(8,128)(2,1)} %copy-done.5), custom_call_target="tpu_custom_call" | custom-call | tf_op jit(solution)/shard_map/auto_csd/pallas_call | solution.py:212
  44.7 0.0 collective-permute-done.7.next_otm_ref
  44.7 0.0 collective-permute-done.8.next_picked_ref
  44.7 0.6 %copy-done.8 = bf16[96,384]{1,0:T(8,128)(2,1)} copy-done((bf16[96,384]{1,0:T(8,128)(2,1)}, bf16[96,384]{1,0:T(8,128)(2,1)S(1)}, u32[]{:S(2)}) %copy-start.8) | copy-done | bytes 73752
  45.4 0.6 %copy-done.7 = bf16[96,512]{1,0:T(8,128)(2,1)} copy-done((bf16[96,512]{1,0:T(8,128)(2,1)}, bf16[96,512]{1,0:T(8,128)(2,1)S(1)}, u32[]{:S(2)}) %copy-start.7) | copy-done | bytes 98328
  46.0 3.9 %joint_csd.1 = bf16[1,4,2,128,384]{4,3,2,1,0:T(8,128)(2,1)} custom-call(s32[1]{0:T(128)} %copy.10.count_ref, bf16[96,384]{1,0:T(8,128)(2,1)} %bitcast.9, bf16[96,512]{1,0:T(8,128)(2,1)} %copy-done.5, bf16[96,384]{1,0:T(8,128)(2,1)} %copy-done.8, bf16[96,512]{1,0:T(8,128)(2,1)} %copy-done.7), custom_call_target="tpu_custom_call" | custom-call | tf_op jit(solution)/shard_map/joint_csd/pallas_call | solution.py:220
  (14 shorter events, 0.0 us)
Async XLA Ops:
  2.0 2.3 %copy-start = (bf16[6144,384]{1,0:T(8,128)(2,1)S(1)}, bf16[6144,384]{1,0:T(8,128)(2,1)}, u32[]{:S(2)}) copy-start(bf16[6144,384]{1,0:T(8,128)(2,1)} %shapes_ref.3) | copy-start | bytes 14155780
  4.3 1.1 %copy-start.2 = (f32[384,4,2,64]{0,3,2,1:T(8,128)S(1)}, f32[384,4,2,64]{0,3,2,1:T(8,128)}, u32[]{:S(2)}) copy-start(f32[384,4,2,64]{0,3,2,1:T(8,128)} %param.12) | copy-start | bytes 2359300
  5.5 0.7 %copy-start.3 = (s32[8,96]{1,0:T(8,128)S(1)}, s32[8,96]{1,0:T(8,128)}, u32[]{:S(2)}) copy-start(s32[8,96]{1,0:T(8,128)} %attach_ref.3) | copy-start | bytes 9220
  6.2 0.7 %copy-start.4 = (f32[4]{0:T(128)S(1)}, f32[4]{0:T(128)}, u32[]{:S(2)}) copy-start(f32[4]{0:T(128)} %exc_ref.1) | copy-start | bytes 52
  6.8 10.1 %copy-start.1 = (bf16[6144,384]{1,0:T(8,128)(2,1)S(1)}, bf16[6144,384]{1,0:T(8,128)(2,1)}, u32[]{:S(2)}) copy-start(bf16[6144,384]{1,0:T(8,128)(2,1)} %shapes_ref.3) | copy-start | bytes 14155780
  6.8 30.5 %copy-start.6 = (bf16[1,384,96]{1,2,0:T(8,128)(2,1)S(1)}, bf16[1,384,96]{1,2,0:T(8,128)(2,1)}, u32[]{:S(2)}) copy-start(bf16[1,384,96]{1,2,0:T(8,128)(2,1)} %param.15) | copy-start | bytes 221188
  13.4 13.8 %collective-permute-start.3 = (bf16[96,512]{1,0:T(8,128)(2,1)S(1)}, bf16[96,512]{1,0:T(8,128)(2,1)S(1)}, u32[]{:S(2)}, u32[]{:S(2)}) collective-permute-start(bf16[96,512]{1,0:T(8,128)(2,1)S(1)} %get-tuple-element.17), channel_id=1, source_target_pairs={{0,1},{1,0},{2,3},{3,2},{4,5},{5,4},{6,7},{7,6},{8,9},{9,8},{10,11... | collective-permute-start | bytes 294920 | tf_op jit(solution)/shard_map/ppermute | solution.py:192
  15.0 12.7 %collective-permute-start.4 = (bf16[96,512]{1,0:T(8,128)(2,1)S(1)}, bf16[96,512]{1,0:T(8,128)(2,1)S(1)}, u32[]{:S(2)}, u32[]{:S(2)}) collective-permute-start(bf16[96,512]{1,0:T(8,128)(2,1)S(1)} %get-tuple-element.18), channel_id=1, source_target_pairs={{0,2},{1,3},{2,0},{3,1},{4,6},{5,7},{6,4},{7,5},{8,10},{9,11},{10,... | collective-permute-start | bytes 294920 | tf_op jit(solution)/shard_map/ppermute | solution.py:192
  16.6 11.1 %collective-permute-start.5 = (bf16[96,512]{1,0:T(8,128)(2,1)S(1)}, bf16[96,512]{1,0:T(8,128)(2,1)S(1)}, u32[]{:S(2)}, u32[]{:S(2)}) collective-permute-start(bf16[96,512]{1,0:T(8,128)(2,1)S(1)} %get-tuple-element.19), channel_id=1, source_target_pairs={{0,3},{1,2},{2,1},{3,0},{4,7},{5,6},{6,5},{7,4},{8,11},{9,10},{10,... | collective-permute-start | bytes 294920 | tf_op jit(solution)/shard_map/ppermute | solution.py:192
  23.4 4.7 %collective-permute-start = (bf16[96,512]{1,0:T(8,128)(2,1)S(1)}, bf16[96,512]{1,0:T(8,128)(2,1)S(1)}, u32[]{:S(2)}, u32[]{:S(2)}) collective-permute-start(bf16[96,512]{1,0:T(8,128)(2,1)S(1)} %get-tuple-element.13), channel_id=1, source_target_pairs={{0,1},{1,0},{2,3},{3,2},{4,5},{5,4},{6,7},{7,6},{8,9},{9,8},{10,11... | collective-permute-start | bytes 294920 | tf_op jit(solution)/shard_map/ppermute | solution.py:192
  24.9 5.7 %collective-permute-start.1 = (bf16[96,512]{1,0:T(8,128)(2,1)S(1)}, bf16[96,512]{1,0:T(8,128)(2,1)S(1)}, u32[]{:S(2)}, u32[]{:S(2)}) collective-permute-start(bf16[96,512]{1,0:T(8,128)(2,1)S(1)} %get-tuple-element.14), channel_id=1, source_target_pairs={{0,2},{1,3},{2,0},{3,1},{4,6},{5,7},{6,4},{7,5},{8,10},{9,11},{10,... | collective-permute-start | bytes 294920 | tf_op jit(solution)/shard_map/ppermute | solution.py:192
  27.2 5.6 %collective-permute-start.2 = (bf16[96,512]{1,0:T(8,128)(2,1)S(1)}, bf16[96,512]{1,0:T(8,128)(2,1)S(1)}, u32[]{:S(2)}, u32[]{:S(2)}) collective-permute-start(bf16[96,512]{1,0:T(8,128)(2,1)S(1)} %get-tuple-element.15), channel_id=1, source_target_pairs={{0,3},{1,2},{2,1},{3,0},{4,7},{5,6},{6,5},{7,4},{8,11},{9,10},{10,... | collective-permute-start | bytes 294920 | tf_op jit(solution)/shard_map/ppermute | solution.py:192
  27.7 5.7 %collective-permute-start.6 = (bf16[96,512]{1,0:T(8,128)(2,1)S(1)}, bf16[96,512]{1,0:T(8,128)(2,1)S(1)}, u32[]{:S(2)}, u32[]{:S(2)}) collective-permute-start(bf16[96,512]{1,0:T(8,128)(2,1)S(1)} %add_convert_fusion.1), channel_id=1, source_target_pairs={{0,4},{1,5},{2,6},{3,7},{4,0},{5,1},{6,2},{7,3},{8,12},{9,13},{10,... | collective-permute-start | bytes 294920 | tf_op jit(solution)/shard_map/ppermute | solution.py:192
  33.4 6.9 %copy-start.5 = (bf16[96,512]{1,0:T(8,128)(2,1)}, bf16[96,512]{1,0:T(8,128)(2,1)S(1)}, u32[]{:S(2)}) copy-start(bf16[96,512]{1,0:T(8,128)(2,1)S(1)} %add_convert_fusion.picked_ref) | copy-start | bytes 294916
  33.5 11.3 %collective-permute-start.8 = (bf16[96,512]{1,0:T(8,128)(2,1)S(1)}, bf16[96,512]{1,0:T(8,128)(2,1)S(1)}, u32[]{:S(2)}, u32[]{:S(2)}) collective-permute-start(bf16[96,512]{1,0:T(8,128)(2,1)S(1)} %add_convert_fusion.picked_ref), channel_id=1, source_target_pairs={{1,0},{2,1},{3,2},{4,3},{5,4},{6,5},{7,6},{9,8},{10,9},{11,10},{12... | collective-permute-start | bytes 294920 | tf_op jit(solution)/shard_map/ppermute | solution.py:195
  37.3 7.4 %collective-permute-start.7 = (bf16[96,384]{1,0:T(8,128)(2,1)S(1)}, bf16[96,384]{1,0:T(8,128)(2,1)S(1)}, u32[]{:S(2)}, u32[]{:S(2)}) collective-permute-start(bf16[96,384]{1,0:T(8,128)(2,1)S(1)} %broadcast_select_fusion), channel_id=1, source_target_pairs={{1,0},{2,1},{3,2},{4,3},{5,4},{6,5},{7,6},{9,8},{10,9},{11,10},{12... | collective-permute-start | bytes 221192 | tf_op jit(solution)/shard_map/ppermute | solution.py:195
  44.7 0.6 %copy-start.8 = (bf16[96,384]{1,0:T(8,128)(2,1)}, bf16[96,384]{1,0:T(8,128)(2,1)S(1)}, u32[]{:S(2)}) copy-start(bf16[96,384]{1,0:T(8,128)(2,1)S(1)} %collective-permute-done.7.next_otm_ref) | copy-start | bytes 221188
  45.4 0.6 %copy-start.7 = (bf16[96,512]{1,0:T(8,128)(2,1)}, bf16[96,512]{1,0:T(8,128)(2,1)S(1)}, u32[]{:S(2)}) copy-start(bf16[96,512]{1,0:T(8,128)(2,1)S(1)} %collective-permute-done.8.next_picked_ref) | copy-start | bytes 294916

commit v2 on v1

v2 whole, which is shorter than its diff:
```python
import functools

import jax
import jax.numpy as jnp
from jax import lax
from jax.experimental import pallas as pl
from jax.experimental.pallas import tpu as pltpu
from jax.sharding import PartitionSpec as P

CROSS = 128
CHUNKS = 6
LANES = 128
F32 = jnp.float32
BF16 = jnp.bfloat16
NT = (((1,), (1,)), ((), ()))
TN = (((0,), (0,)), ((), ()))


def modal_response(freq_ref, damp_ref, exc_ref, load_ref, resp_ref):
    lines = load_ref.shape[0]
    width = load_ref.shape[2]
    freq = freq_ref[...].reshape(1, -1)
    damp = damp_ref[...].reshape(1, -1)
    omega_sq = freq * freq
    for f in range(lines):
        exc = exc_ref[f]
        a = omega_sq - exc * exc
        b = 2.0 * damp * freq * exc
        denom = a * a + b * b
        frf_re = omega_sq * a / denom
        frf_im = -omega_sq * b / denom
        load_re = load_ref[f, 0]
        load_im = load_ref[f, 1]
        base = f * 2 * width
        resp_ref[base : base + width, :] = (frf_re * load_re - frf_im * load_im).astype(BF16)
        resp_ref[base + width : base + 2 * width, :] = (
            frf_re * load_im + frf_im * load_re
        ).astype(BF16)


def parts_kernel(
    slots, attach_hbm, exc_hbm, count_hbm, freq_hbm, damp_hbm, load_hbm, otm_hbm, shapes_hbm, *rest
):
    outs = rest[: len(slots)]
    otm_ref = rest[len(slots)]
    (attach, exc, rows_here, freq, damp, load, otm, raw, wide, picks, resp, sems, small) = rest[
        len(slots) + 1 :
    ]
    copies = [
        pltpu.make_async_copy(source, target, small.at[i])
        for i, (source, target) in enumerate(
            [
                (freq_hbm, freq),
                (damp_hbm, damp),
                (exc_hbm, exc),
                (load_hbm, load),
                (attach_hbm, attach),
                (count_hbm, rows_here),
                (otm_hbm, otm),
            ]
        )
    ]
    for copy in copies:
        copy.start()
    chunks = sems.shape[0]
    step = raw.shape[0] // chunks
    pieces = raw.shape[1] // LANES
    att = picks.shape[0] // (len(slots) * pieces)

    def fetch(i):
        rows = pl.ds(pl.multiple_of(i * step, step), step)
        return pltpu.make_async_copy(shapes_hbm.at[rows, :], raw.at[rows, :], sems.at[i])

    for i in range(chunks):
        fetch(i).start()
    for copy in copies:
        copy.wait()
    modal_response(freq, damp, exc, load, resp)
    lane = lax.broadcasted_iota(jnp.int32, otm.shape, 1)
    otm_ref[...] = jnp.where(lane < rows_here[0], otm[...], jnp.zeros_like(otm))

    def widen(i, carry):
        fetch(i).wait()
        first = pl.multiple_of(i * step, step)
        for k in range(pieces):
            block = raw[pl.ds(first, step), k * LANES : (k + 1) * LANES]
            wide[pl.ds(first * pieces + k, step, stride=pieces), :] = block.astype(F32)
        return carry

    lax.fori_loop(0, chunks, widen, 0)
    me = lax.axis_index("mode")

    def pick(slot, first):
        comp = jnp.bitwise_xor(me, slot)
        rows = [wide[pl.ds(attach[comp, a] * pieces, pieces), :] for a in range(att)]
        for a in range(att):
            picks[pl.ds(first + a * pieces, pieces), :] = rows[a]

    for i, slot in enumerate(slots):
        pick(slot, i * att * pieces)
    group = min(8, len(slots))
    for start in range(0, len(slots), group):
        count = group * att
        lhs = jnp.concatenate(
            [
                picks[pl.ds(start * att * pieces + k, count, stride=pieces), :].astype(BF16)
                for k in range(pieces)
            ],
            axis=1,
        )
        part = lax.dot_general(lhs, resp[...], NT, preferred_element_type=F32)
        for i in range(group):
            out = outs[start + i]
            out[...] = part[i * att : (i + 1) * att].astype(out.dtype)


def turned(z):
    width = z.shape[1] // 2
    return jnp.concatenate([z[:, width:], -z[:, :width]], axis=1)


def spectra(left, right, out_hbm, buffer, sems, f):
    pair = left.shape[1]
    rows = left.shape[0]
    both = jnp.concatenate([left, turned(left)], axis=0)
    value = lax.dot_general(both, right, NT, preferred_element_type=F32) * (2.0 / pair)
    value = value.astype(BF16)
    buffer[f, 0] = value[:rows]
    buffer[f, 1] = value[rows:]
    copy = pltpu.make_async_copy(buffer.at[f], out_hbm.at[0, f], sems.at[f])
    copy.start()
    return copy


def auto_kernel(otm_ref, picked_ref, csd_hbm, left_ref, buffer, sems):
    lines = buffer.shape[0]
    cross = left_ref.shape[0]
    z = lax.dot_general(otm_ref[...], picked_ref[...], TN, preferred_element_type=F32)
    z = z.astype(BF16)
    pair = z.shape[1] // lines
    left_ref[...] = z[:cross]
    copies = []
    for f in range(lines):
        line = z[:, f * pair : (f + 1) * pair]
        copies.append(spectra(line, line, csd_hbm, buffer, sems, f))
    for copy in copies:
        copy.wait()


def joint_kernel(left_ref, otm_ref, picked_ref, joint_hbm, buffer, sems):
    lines = buffer.shape[0]
    z = lax.dot_general(otm_ref[...], picked_ref[...], TN, preferred_element_type=F32)
    z = z.astype(BF16)
    pair = z.shape[1] // lines
    copies = []
    for f in range(lines):
        columns = slice(f * pair, (f + 1) * pair)
        copies.append(
            spectra(left_ref[:, columns], z[:, columns], joint_hbm, buffer, sems, f)
        )
    for copy in copies:
        copy.wait()


def per_device(mode_shapes, modal_freq, damping, excitation, modal_load, attach, row_count, otm):
    count = lax.axis_size("mode")
    half = count // 2
    iface, modes = mode_shapes.shape
    rows_max, att = otm.shape[1], otm.shape[2]
    lines = excitation.shape[0]
    pair = 2 * modal_load.shape[3]
    columns = lines * pair
    vmem = pl.BlockSpec(memory_space=pltpu.VMEM)
    hbm = pl.BlockSpec(memory_space=pl.ANY)
    load_t = jnp.transpose(modal_load, (1, 2, 3, 0))
    otm_t = jnp.transpose(otm[0], (1, 0))
    part = jax.ShapeDtypeStruct((att, columns), BF16)
    part_wide = jax.ShapeDtypeStruct((att, columns), F32)
    chunks = CHUNKS if iface % (16 * CHUNKS) == 0 else 1
    pieces = modes // LANES
    steps = list(range(1, half))
    slots = [half ^ k for k in steps] + [half] + steps + [0]
    outs = pl.pallas_call(
        functools.partial(parts_kernel, slots),
        out_shape=([part] * (half - 1) + [part_wide]) * 2
        + [jax.ShapeDtypeStruct(otm_t.shape, BF16)],
        in_specs=[hbm] * 8,
        out_specs=[vmem] * (count + 1),
        scratch_shapes=[
            pltpu.SMEM(attach.shape, jnp.int32),
            pltpu.SMEM(excitation.shape, F32),
            pltpu.SMEM(row_count.shape, jnp.int32),
            pltpu.VMEM(modal_freq.shape, F32),
            pltpu.VMEM(damping.shape, F32),
            pltpu.VMEM(load_t.shape, F32),
            pltpu.VMEM(otm_t.shape, BF16),
            pltpu.VMEM((iface, modes), BF16),
            pltpu.VMEM((iface * pieces, LANES), F32),
            pltpu.VMEM((count * att * pieces, LANES), F32),
            pltpu.VMEM((columns, modes), BF16),
            pltpu.SemaphoreType.DMA((chunks,)),
            pltpu.SemaphoreType.DMA((7,)),
        ],
        compiler_params=pltpu.CompilerParams(vmem_limit_bytes=60 << 20),
        name="partial_sums",
    )(attach, excitation, row_count, modal_freq, damping, load_t, otm_t, mode_shapes)
    far, far_own = outs[: half - 1], outs[half - 1]
    near, near_own = outs[half : count - 1], outs[count - 1]
    own_otm = outs[count]

    def swapped(value, k):
        return lax.ppermute(value, "mode", [(i, i ^ k) for i in range(count)])

    def following(value):
        return lax.ppermute(value, "mode", [(i, i - 1) for i in range(1, count)])

    far_sum = far_own
    for k, value in zip(steps, far):
        far_sum = far_sum + swapped(value, k).astype(F32)
    picked = near_own
    for k, value in zip(steps, near):
        picked = picked + swapped(value, k).astype(F32)
    picked = picked + swapped(far_sum.astype(BF16), half).astype(F32)
    picked = picked.astype(BF16)
    next_otm = following(own_otm)
    next_picked = following(picked)

    params = pltpu.CompilerParams(vmem_limit_bytes=24 << 20)
    csd, left = pl.pallas_call(
        auto_kernel,
        out_shape=[
            jax.ShapeDtypeStruct((1, lines, 2, rows_max, rows_max), BF16),
            jax.ShapeDtypeStruct((CROSS, columns), BF16),
        ],
        in_specs=[vmem] * 2,
        out_specs=[hbm, vmem],
        scratch_shapes=[
            pltpu.VMEM((lines, 2, rows_max, rows_max), BF16),
            pltpu.SemaphoreType.DMA((lines,)),
        ],
        compiler_params=params,
        name="auto_csd",
    )(own_otm, picked)
    joint = pl.pallas_call(
        joint_kernel,
        out_shape=jax.ShapeDtypeStruct((1, lines, 2, CROSS, rows_max), BF16),
        in_specs=[vmem] * 3,
        out_specs=hbm,
        scratch_shapes=[
            pltpu.VMEM((lines, 2, CROSS, rows_max), BF16),
            pltpu.SemaphoreType.DMA((lines,)),
        ],
        compiler_params=params,
        name="joint_csd",
    )(left, next_otm, next_picked)
    return (csd, joint)


def solution(mesh):
    return jax.shard_map(
        per_device,
        mesh=mesh,
        in_specs=(
            P(None, "mode"),
            P("mode"),
            P("mode"),
            P("freq"),
            P("mode", "freq", None, None),
            P(),
            P("mode"),
            P("mode", None, None),
        ),
        out_specs=(P("mode", "freq", None, None, None), P("mode", "freq", None, None, None)),
        check_vma=False,
    )
```

time: 50.6 us -> 36.7 us (0.73)
  the two profiles are of different devices: /device:TPU:16 before, /device:TPU:0 now
where the time goes in v2:
time: 36.7 us; the launch traced here: 36.4 us
  starting transfers between devices  14.2 us (39%)
  waiting for transfers between devices  9.39 us (26%)
  Pallas kernels  8.67 us (24%)
  other arithmetic  1.97 us (5%)
  between operations  1.33 us (4%)
  local copies, waits for them, and re-layouts  0.88 us (2%)
    ppermute x7, starting transfers between devices, swapped(): return lax.ppermute(value, 'mode', [(i, i ^ k) for i in range(count)])  11.6 us
    ppermute x7, waiting for transfers between devices, swapped(): return lax.ppermute(value, 'mode', [(i, i ^ k) for i in range(count)])  6.51 us
    pallas_call x1, Pallas kernels, per_device(): pl.pallas_call(functools.partial(parts_kernel, slots), out_shape=([part]...  5.29 us
    ppermute x2, waiting for transfers between devices, following(): return lax.ppermute(value, 'mode', [(i, i - 1) for i in range(1, count)])  2.89 us
    ppermute x2, starting transfers between devices, following(): return lax.ppermute(value, 'mode', [(i, i - 1) for i in range(1, count)])  2.58 us
    pallas_call x1, Pallas kernels, per_device(): pl.pallas_call(auto_kernel, out_shape=[jax.ShapeDtypeStruct((1, lines, 2,...  2.01 us
    pallas_call x1, Pallas kernels, per_device(): pl.pallas_call(joint_kernel, out_shape=jax.ShapeDtypeStruct((1, lines, 2,...  1.37 us
    convert_element_type x1, other arithmetic, per_device(): picked = picked.astype(BF16)  0.99 us
  transfers between devices with their start and end apart: 9, of which 3 were waited for; matrix products, arithmetic and copies ran while one was open for 3% of the time, Pallas kernels for 6%

profile of v2, /device:TPU:0, one launch (start us, length us, event | category | flops | bytes accessed | tf_op | source)
XLA Modules:
  0.0 36.4 jit_solution(5741350849974890941)
XLA Ops:
  1.3 5.3 %partial_sums.1 = (bf16[96,512]{1,0:T(8,128)(2,1)}, bf16[96,512]{1,0:T(8,128)(2,1)}, bf16[96,512]{1,0:T(8,128)(2,1)}, f32[96,512]{1,0:T(8,128)}, bf16[96,512]{1,...) custom-call(s32[8,96]{1,0:T(8,128)} %attach_hbm.1, ...), custom_call_target="tpu_custom_call" | custom-call | tf_op jit(solution)/shard_map/partial_sums/pallas_call | solution.py:183
  6.6 3.0 %collective-permute-start.3 = (bf16[96,512]{1,0:T(8,128)(2,1)}, bf16[96,512]{1,0:T(8,128)(2,1)S(1)}, u32[]{:S(2)}, u32[]{:S(2)}) collective-permute-start(bf16[96,512]{1,0:T(8,128)(2,1)} %get-tuple-element.19), channel_id=1, source_target_pairs={{0,1},{1,0},{2,3},{3,2},{4,5},{5,4},{6,7},{7,6},{8,9},{9,8},{10,11... | collective-permute-start | bytes 294920 | tf_op jit(solution)/shard_map/ppermute | solution.py:212
  9.6 1.6 %collective-permute-start.4 = (bf16[96,512]{1,0:T(8,128)(2,1)}, bf16[96,512]{1,0:T(8,128)(2,1)S(1)}, u32[]{:S(2)}, u32[]{:S(2)}) collective-permute-start(bf16[96,512]{1,0:T(8,128)(2,1)} %get-tuple-element.20), channel_id=1, source_target_pairs={{0,2},{1,3},{2,0},{3,1},{4,6},{5,7},{6,4},{7,5},{8,10},{9,11},{10,... | collective-permute-start | bytes 294920 | tf_op jit(solution)/shard_map/ppermute | solution.py:212
  11.2 0.0 collective-permute-start.5
  11.2 1.9 %collective-permute-start = (bf16[96,512]{1,0:T(8,128)(2,1)}, bf16[96,512]{1,0:T(8,128)(2,1)S(1)}, u32[]{:S(2)}, u32[]{:S(2)}) collective-permute-start(bf16[96,512]{1,0:T(8,128)(2,1)} %get-tuple-element.15), channel_id=1, source_target_pairs={{0,1},{1,0},{2,3},{3,2},{4,5},{5,4},{6,7},{7,6},{8,9},{9,8},{10,11... | collective-permute-start | bytes 294920 | tf_op jit(solution)/shard_map/ppermute | solution.py:212
  13.1 1.6 %collective-permute-start.1 = (bf16[96,512]{1,0:T(8,128)(2,1)}, bf16[96,512]{1,0:T(8,128)(2,1)S(1)}, u32[]{:S(2)}, u32[]{:S(2)}) collective-permute-start(bf16[96,512]{1,0:T(8,128)(2,1)} %get-tuple-element.16), channel_id=1, source_target_pairs={{0,2},{1,3},{2,0},{3,1},{4,6},{5,7},{6,4},{7,5},{8,10},{9,11},{10,... | collective-permute-start | bytes 294920 | tf_op jit(solution)/shard_map/ppermute | solution.py:212
  14.7 0.0 collective-permute-done.3
  14.7 0.8 %collective-permute-start.2 = (bf16[96,512]{1,0:T(8,128)(2,1)}, bf16[96,512]{1,0:T(8,128)(2,1)S(1)}, u32[]{:S(2)}, u32[]{:S(2)}) collective-permute-start(bf16[96,512]{1,0:T(8,128)(2,1)} %get-tuple-element.17), channel_id=1, source_target_pairs={{0,3},{1,2},{2,1},{3,0},{4,7},{5,6},{6,5},{7,4},{8,11},{9,10},{10,... | collective-permute-start | bytes 294920 | tf_op jit(solution)/shard_map/ppermute | solution.py:212
  15.5 0.0 collective-permute-done.4
  15.5 2.5 %collective-permute-done.5 = bf16[96,512]{1,0:T(8,128)(2,1)S(1)} collective-permute-done((bf16[96,512]{1,0:T(8,128)(2,1)}, bf16[96,512]{1,0:T(8,128)(2,1)S(1)}, u32[]{:S(2)}, u32[]{:S(2)}) %collective-permute-start.5) | collective-permute-done | bytes 98336 | tf_op jit(solution)/shard_map/ppermute | solution.py:212
  18.0 1.0 %add_convert_fusion.1 = bf16[96,512]{1,0:T(8,128)(2,1)S(1)} fusion(bf16[96,512]{1,0:T(8,128)(2,1)S(1)} %collective-permute-done.5, bf16[96,512]{1,0:T(8,128)(2,1)S(1)} %collective-permute-done.4, f32[96,512]{1,0:T(8,128)} %get-tuple-element.18, bf16[96,512]{1,0:T(8,128)(2,1)S(1)} %collective-permute-done.3), kind=kLoop, calls=%fused_computation.1 | loop fusion | flops 344064 | bytes 589824 | tf_op jit(solution)/shard_map/convert_element_type | solution.py:223
  19.0 2.7 %collective-permute-start.6 = (bf16[96,512]{1,0:T(8,128)(2,1)S(1)}, bf16[96,512]{1,0:T(8,128)(2,1)S(1)}, u32[]{:S(2)}, u32[]{:S(2)}) collective-permute-start(bf16[96,512]{1,0:T(8,128)(2,1)S(1)} %add_convert_fusion.1), channel_id=1, source_target_pairs={{0,4},{1,5},{2,6},{3,7},{4,0},{5,1},{6,2},{7,3},{8,12},{9,13},{10,... | collective-permute-start | bytes 294920 | tf_op jit(solution)/shard_map/ppermute | solution.py:212
  21.7 0.0 collective-permute-done
  21.7 0.0 collective-permute-done.1
  21.7 0.0 collective-permute-done.2
  21.7 3.9 %collective-permute-done.6 = bf16[96,512]{1,0:T(8,128)(2,1)S(1)} collective-permute-done((bf16[96,512]{1,0:T(8,128)(2,1)S(1)}, bf16[96,512]{1,0:T(8,128)(2,1)S(1)}, u32[]{:S(2)}, u32[]{:S(2)}) %collective-permute-start.6) | collective-permute-done | bytes 98336 | tf_op jit(solution)/shard_map/ppermute | solution.py:212
  25.6 1.0 %add_convert_fusion.picked_ref = bf16[96,512]{1,0:T(8,128)(2,1)S(1)} fusion(bf16[96,512]{1,0:T(8,128)(2,1)S(1)} %collective-permute-done.6, bf16[96,512]{1,0:T(8,128)(2,1)S(1)} %collective-permute-done.2, bf16[96,512]{1,0:T(8,128)(2,1)S(1)} %collective-permute-done.1, f32[96,512]{1,0:T(8,128)} %get-tuple-element.14, bf16[96,512]{1,0:T(8,128)(2,1)S(1)} %collective-permute-done), kind=kLoop, calls=%fused_computation | loop fusion | flops 442368 | bytes 688128 | tf_op jit(solution)/shard_map/convert_element_type | solution.py:224
  26.6 1.3 %collective-permute-start.8 = (bf16[96,512]{1,0:T(8,128)(2,1)S(1)}, bf16[96,512]{1,0:T(8,128)(2,1)S(1)}, u32[]{:S(2)}, u32[]{:S(2)}) collective-permute-start(bf16[96,512]{1,0:T(8,128)(2,1)S(1)} %add_convert_fusion.picked_ref), channel_id=1, source_target_pairs={{1,0},{2,1},{3,2},{4,3},{5,4},{6,5},{7,6},{9,8},{10,9},{11,10},{12... | collective-permute-start | bytes 294920 | tf_op jit(solution)/shard_map/ppermute | solution.py:215
  27.9 1.3 %collective-permute-start.7 = (bf16[96,384]{1,0:T(8,128)(2,1)}, bf16[96,384]{1,0:T(8,128)(2,1)S(1)}, u32[]{:S(2)}, u32[]{:S(2)}) collective-permute-start(bf16[96,384]{1,0:T(8,128)(2,1)} %get-tuple-element.13.otm_ref), channel_id=1, source_target_pairs={{1,0},{2,1},{3,2},{4,3},{5,4},{6,5},{7,6},{9,8},{10,9},{11,10},{12... | collective-permute-start | bytes 221192 | tf_op jit(solution)/shard_map/ppermute | solution.py:215
  29.2 0.0 copy-start
  29.3 0.9 %copy-done = bf16[96,384]{1,0:T(8,128)(2,1)S(1)} copy-done((bf16[96,384]{1,0:T(8,128)(2,1)S(1)}, bf16[96,384]{1,0:T(8,128)(2,1)}, u32[]{:S(2)}) %copy-start) | copy-done | bytes 73752
  30.1 2.0 %auto_csd.1 = (bf16[1,4,2,384,384]{4,3,2,1,0:T(8,128)(2,1)}, bf16[128,512]{1,0:T(8,128)(2,1)S(1)}) custom-call(bf16[96,384]{1,0:T(8,128)(2,1)S(1)} %copy-done, bf16[96,512]{1,0:T(8,128)(2,1)S(1)} %add_convert_fusion.picked_ref), custom_call_target="tpu_custom_call" | custom-call | tf_op jit(solution)/shard_map/auto_csd/pallas_call | solution.py:229
  32.1 2.9 %collective-permute-done.7.otm_ref = bf16[96,384]{1,0:T(8,128)(2,1)S(1)} collective-permute-done((bf16[96,384]{1,0:T(8,128)(2,1)}, bf16[96,384]{1,0:T(8,128)(2,1)S(1)}, u32[]{:S(2)}, u32[]{:S(2)}) %collective-permute-start.7) | collective-permute-done | bytes 73760 | tf_op jit(solution)/shard_map/ppermute | solution.py:215
  35.0 0.0 collective-permute-done.8.picked_ref
  35.0 1.4 %joint_csd.1 = bf16[1,4,2,128,384]{4,3,2,1,0:T(8,128)(2,1)} custom-call(bf16[128,512]{1,0:T(8,128)(2,1)S(1)} %get-tuple-element.23.left_ref, bf16[96,384]{1,0:T(8,128)(2,1)S(1)} %collective-permute-done.7.otm_ref, bf16[96,512]{1,0:T(8,128)(2,1)S(1)} %collective-permute-done.8.picked_ref), custom_call_target="tpu_custom_call" | custom-call | tf_op jit(solution)/shard_map/joint_csd/pallas_call | solution.py:244
Async XLA Ops:
  6.6 8.1 %collective-permute-start.3 = (bf16[96,512]{1,0:T(8,128)(2,1)}, bf16[96,512]{1,0:T(8,128)(2,1)S(1)}, u32[]{:S(2)}, u32[]{:S(2)}) collective-permute-start(bf16[96,512]{1,0:T(8,128)(2,1)} %get-tuple-element.19), channel_id=1, source_target_pairs={{0,1},{1,0},{2,3},{3,2},{4,5},{5,4},{6,7},{7,6},{8,9},{9,8},{10,11... | collective-permute-start | bytes 294920 | tf_op jit(solution)/shard_map/ppermute | solution.py:212
  9.6 5.9 %collective-permute-start.4 = (bf16[96,512]{1,0:T(8,128)(2,1)}, bf16[96,512]{1,0:T(8,128)(2,1)S(1)}, u32[]{:S(2)}, u32[]{:S(2)}) collective-permute-start(bf16[96,512]{1,0:T(8,128)(2,1)} %get-tuple-element.20), channel_id=1, source_target_pairs={{0,2},{1,3},{2,0},{3,1},{4,6},{5,7},{6,4},{7,5},{8,10},{9,11},{10,... | collective-permute-start | bytes 294920 | tf_op jit(solution)/shard_map/ppermute | solution.py:212
  11.2 6.8 %collective-permute-start.5 = (bf16[96,512]{1,0:T(8,128)(2,1)}, bf16[96,512]{1,0:T(8,128)(2,1)S(1)}, u32[]{:S(2)}, u32[]{:S(2)}) collective-permute-start(bf16[96,512]{1,0:T(8,128)(2,1)} %get-tuple-element.21), channel_id=1, source_target_pairs={{0,3},{1,2},{2,1},{3,0},{4,7},{5,6},{6,5},{7,4},{8,11},{9,10},{10,... | collective-permute-start | bytes 294920 | tf_op jit(solution)/shard_map/ppermute | solution.py:212
  11.2 10.5 %collective-permute-start = (bf16[96,512]{1,0:T(8,128)(2,1)}, bf16[96,512]{1,0:T(8,128)(2,1)S(1)}, u32[]{:S(2)}, u32[]{:S(2)}) collective-permute-start(bf16[96,512]{1,0:T(8,128)(2,1)} %get-tuple-element.15), channel_id=1, source_target_pairs={{0,1},{1,0},{2,3},{3,2},{4,5},{5,4},{6,7},{7,6},{8,9},{9,8},{10,11... | collective-permute-start | bytes 294920 | tf_op jit(solution)/shard_map/ppermute | solution.py:212
  13.1 8.6 %collective-permute-start.1 = (bf16[96,512]{1,0:T(8,128)(2,1)}, bf16[96,512]{1,0:T(8,128)(2,1)S(1)}, u32[]{:S(2)}, u32[]{:S(2)}) collective-permute-start(bf16[96,512]{1,0:T(8,128)(2,1)} %get-tuple-element.16), channel_id=1, source_target_pairs={{0,2},{1,3},{2,0},{3,1},{4,6},{5,7},{6,4},{7,5},{8,10},{9,11},{10,... | collective-permute-start | bytes 294920 | tf_op jit(solution)/shard_map/ppermute | solution.py:212
  14.7 7.0 %collective-permute-start.2 = (bf16[96,512]{1,0:T(8,128)(2,1)}, bf16[96,512]{1,0:T(8,128)(2,1)S(1)}, u32[]{:S(2)}, u32[]{:S(2)}) collective-permute-start(bf16[96,512]{1,0:T(8,128)(2,1)} %get-tuple-element.17), channel_id=1, source_target_pairs={{0,3},{1,2},{2,1},{3,0},{4,7},{5,6},{6,5},{7,4},{8,11},{9,10},{10,... | collective-permute-start | bytes 294920 | tf_op jit(solution)/shard_map/ppermute | solution.py:212
  19.0 6.6 %collective-permute-start.6 = (bf16[96,512]{1,0:T(8,128)(2,1)S(1)}, bf16[96,512]{1,0:T(8,128)(2,1)S(1)}, u32[]{:S(2)}, u32[]{:S(2)}) collective-permute-start(bf16[96,512]{1,0:T(8,128)(2,1)S(1)} %add_convert_fusion.1), channel_id=1, source_target_pairs={{0,4},{1,5},{2,6},{3,7},{4,0},{5,1},{6,2},{7,3},{8,12},{9,13},{10,... | collective-permute-start | bytes 294920 | tf_op jit(solution)/shard_map/ppermute | solution.py:212
  26.6 8.4 %collective-permute-start.8 = (bf16[96,512]{1,0:T(8,128)(2,1)S(1)}, bf16[96,512]{1,0:T(8,128)(2,1)S(1)}, u32[]{:S(2)}, u32[]{:S(2)}) collective-permute-start(bf16[96,512]{1,0:T(8,128)(2,1)S(1)} %add_convert_fusion.picked_ref), channel_id=1, source_target_pairs={{1,0},{2,1},{3,2},{4,3},{5,4},{6,5},{7,6},{9,8},{10,9},{11,10},{12... | collective-permute-start | bytes 294920 | tf_op jit(solution)/shard_map/ppermute | solution.py:215
  27.9 7.1 %collective-permute-start.7 = (bf16[96,384]{1,0:T(8,128)(2,1)}, bf16[96,384]{1,0:T(8,128)(2,1)S(1)}, u32[]{:S(2)}, u32[]{:S(2)}) collective-permute-start(bf16[96,384]{1,0:T(8,128)(2,1)} %get-tuple-element.13.otm_ref), channel_id=1, source_target_pairs={{1,0},{2,1},{3,2},{4,3},{5,4},{6,5},{7,6},{9,8},{10,9},{11,10},{12... | collective-permute-start | bytes 221192 | tf_op jit(solution)/shard_map/ppermute | solution.py:215
  29.2 0.9 %copy-start = (bf16[96,384]{1,0:T(8,128)(2,1)S(1)}, bf16[96,384]{1,0:T(8,128)(2,1)}, u32[]{:S(2)}) copy-start(bf16[96,384]{1,0:T(8,128)(2,1)} %get-tuple-element.13.otm_ref) | copy-start | bytes 221188

commit v3 on v2

--- a/solution.py
+++ b/solution.py
@@ -39,13 +39,10 @@
 
 
 def parts_kernel(
-    slots, attach_hbm, exc_hbm, count_hbm, freq_hbm, damp_hbm, load_hbm, otm_hbm, shapes_hbm, *rest
+    slots, attach_hbm, exc_hbm, freq_hbm, damp_hbm, load_hbm, shapes_hbm, *rest
 ):
     outs = rest[: len(slots)]
-    otm_ref = rest[len(slots)]
-    (attach, exc, rows_here, freq, damp, load, otm, raw, wide, picks, resp, sems, small) = rest[
-        len(slots) + 1 :
-    ]
+    attach, exc, freq, damp, load, raw, wide, picks, resp, sems, small = rest[len(slots) :]
     copies = [
         pltpu.make_async_copy(source, target, small.at[i])
         for i, (source, target) in enumerate(
@@ -55,8 +52,6 @@
                 (exc_hbm, exc),
                 (load_hbm, load),
                 (attach_hbm, attach),
-                (count_hbm, rows_here),
-                (otm_hbm, otm),
             ]
         )
     ]
@@ -76,8 +71,6 @@
     for copy in copies:
         copy.wait()
     modal_response(freq, damp, exc, load, resp)
-    lane = lax.broadcasted_iota(jnp.int32, otm.shape, 1)
-    otm_ref[...] = jnp.where(lane < rows_here[0], otm[...], jnp.zeros_like(otm))
 
     def widen(i, carry):
         fetch(i).wait()
@@ -174,39 +167,37 @@
     hbm = pl.BlockSpec(memory_space=pl.ANY)
     load_t = jnp.transpose(modal_load, (1, 2, 3, 0))
     otm_t = jnp.transpose(otm[0], (1, 0))
-    part = jax.ShapeDtypeStruct((att, columns), BF16)
-    part_wide = jax.ShapeDtypeStruct((att, columns), F32)
+    part = pltpu.VMEM((att, columns), BF16)
+    part_wide = pltpu.VMEM((att, columns), F32)
     chunks = CHUNKS if iface % (16 * CHUNKS) == 0 else 1
     pieces = modes // LANES
-    steps = list(range(1, half))
+    steps = list(range(half - 1, 0, -1))
     slots = [half ^ k for k in steps] + [half] + steps + [0]
     outs = pl.pallas_call(
         functools.partial(parts_kernel, slots),
-        out_shape=([part] * (half - 1) + [part_wide]) * 2
-        + [jax.ShapeDtypeStruct(otm_t.shape, BF16)],
-        in_specs=[hbm] * 8,
-        out_specs=[vmem] * (count + 1),
+        out_shape=([part] * (half - 1) + [part_wide]) * 2,
+        in_specs=[hbm] * 6,
+        out_specs=[vmem] * count,
         scratch_shapes=[
             pltpu.SMEM(attach.shape, jnp.int32),
             pltpu.SMEM(excitation.shape, F32),
-            pltpu.SMEM(row_count.shape, jnp.int32),
             pltpu.VMEM(modal_freq.shape, F32),
             pltpu.VMEM(damping.shape, F32),
             pltpu.VMEM(load_t.shape, F32),
-            pltpu.VMEM(otm_t.shape, BF16),
             pltpu.VMEM((iface, modes), BF16),
             pltpu.VMEM((iface * pieces, LANES), F32),
             pltpu.VMEM((count * att * pieces, LANES), F32),
             pltpu.VMEM((columns, modes), BF16),
             pltpu.SemaphoreType.DMA((chunks,)),
-            pltpu.SemaphoreType.DMA((7,)),
-        ],
-        compiler_params=pltpu.CompilerParams(vmem_limit_bytes=60 << 20),
+            pltpu.SemaphoreType.DMA((5,)),
+        ],
+        compiler_params=pltpu.CompilerParams(vmem_limit_bytes=58 << 20),
         name="partial_sums",
-    )(attach, excitation, row_count, modal_freq, damping, load_t, otm_t, mode_shapes)
-    far, far_own = outs[: half - 1], outs[half - 1]
-    near, near_own = outs[half : count - 1], outs[count - 1]
-    own_otm = outs[count]
+    )(attach, excitation, modal_freq, damping, load_t, mode_shapes)
+    far, far_own = list(outs[: half - 1]), outs[half - 1]
+    near, near_own = list(outs[half : count - 1]), outs[count - 1]
+    used = jnp.arange(rows_max, dtype=jnp.int32)[None, :] < row_count[:, None]
+    own_otm = jnp.where(used, otm_t, jnp.zeros_like(otm_t))
 
     def swapped(value, k):
         return lax.ppermute(value, "mode", [(i, i ^ k) for i in range(count)])
@@ -217,12 +208,13 @@
     far_sum = far_own
     for k, value in zip(steps, far):
         far_sum = far_sum + swapped(value, k).astype(F32)
+    next_otm = following(own_otm)
     picked = near_own
     for k, value in zip(steps, near):
         picked = picked + swapped(value, k).astype(F32)
-    picked = picked + swapped(far_sum.astype(BF16), half).astype(F32)
-    picked = picked.astype(BF16)
-    next_otm = following(own_otm)
+    across = swapped(far_sum.astype(BF16), half)
+    picked, next_otm = lax.optimization_barrier((picked, next_otm))
+    picked = (picked + across.astype(F32)).astype(BF16)
     next_picked = following(picked)
 
     params = pltpu.CompilerParams(vmem_limit_bytes=24 << 20)

time: 36.7 us -> 31.5 us (0.86)
  waiting for transfers between devices: 9.39 us -> 6.31 us
  other arithmetic: 1.97 us -> 0.14 us
  starting transfers between devices: 14.2 us -> 15.8 us
  Pallas kernels: 8.67 us -> 7.66 us
  local copies, waits for them, and re-layouts: 0.88 us -> 0.01 us
    ppermute x7, waiting for transfers between devices: 6.51 us -> 3.13 us  [swapped(): return lax.ppermute(value, 'mode', [(i, i ^ k) for i in range(count)])]
    convert_element_type x2, other arithmetic: 1.97 us -> 0.07 us  [the longest x1 0.05 us: per_device(): across = swapped(far_sum.astype(BF16), half)]
    ppermute x7, starting transfers between devices: 11.6 us -> 13.2 us  [swapped(): return lax.ppermute(value, 'mode', [(i, i ^ k) for i in range(count)])]
    pallas_call x1, Pallas kernels: 5.29 us -> 4.28 us  [per_device(): pl.pallas_call(functools.partial(parts_kernel, slots), out_shape=([part]...]
    unnamed x2, local copies, waits for them, and re-layouts: 0.88 us -> 0.01 us
  transfers between devices with their start and end apart: 9 -> 9, of which waited for: 3 -> 3; matrix products, arithmetic and copies ran while one was open for 3% -> 0% of each run, Pallas kernels for 6% -> 6%
where the time goes in v3:
time: 31.5 us; the launch traced here: 31.3 us
  starting transfers between devices  15.8 us (50%)
  Pallas kernels  7.66 us (24%)
  waiting for transfers between devices  6.31 us (20%)
  between operations  1.37 us (4%)
    ppermute x7, starting transfers between devices, swapped(): return lax.ppermute(value, 'mode', [(i, i ^ k) for i in range(count)])  13.2 us
    pallas_call x1, Pallas kernels, per_device(): pl.pallas_call(functools.partial(parts_kernel, slots), out_shape=([part]...  4.28 us
    ppermute x2, waiting for transfers between devices, following(): return lax.ppermute(value, 'mode', [(i, i - 1) for i in range(1, count)])  3.18 us
    ppermute x7, waiting for transfers between devices, swapped(): return lax.ppermute(value, 'mode', [(i, i ^ k) for i in range(count)])  3.13 us
    ppermute x2, starting transfers between devices, following(): return lax.ppermute(value, 'mode', [(i, i - 1) for i in range(1, count)])  2.58 us
    pallas_call x1, Pallas kernels, per_device(): pl.pallas_call(auto_kernel, out_shape=[jax.ShapeDtypeStruct((1, lines, 2,...  2.02 us
    pallas_call x1, Pallas kernels, per_device(): pl.pallas_call(joint_kernel, out_shape=jax.ShapeDtypeStruct((1, lines, 2,...  1.36 us
  transfers between devices with their start and end apart: 9, of which 3 were waited for; matrix products, arithmetic and copies ran while one was open for 0% of the time, Pallas kernels for 6%

profile of v3, /device:TPU:0, one launch (start us, length us, event | category | flops | bytes accessed | tf_op | source)
XLA Modules:
  0.0 31.3 jit_solution(15753415189881788588)
XLA Ops:
  0.6 0.0 copy-start
  0.6 4.3 %partial_sums.1 = (bf16[96,512]{1,0:T(8,128)(2,1)S(1)}, bf16[96,512]{1,0:T(8,128)(2,1)S(1)}, bf16[96,512]{1,0:T(8,128)(2,1)S(1)}, f32[96,512]{1,0:T(8,128)S(1)},...) custom-call(s32[8,96]{1,0:T(8,128)} %attach_hbm.1, ...), custom_call_target="tpu_custom_call" | custom-call | tf_op jit(solution)/shard_map/partial_sums/pallas_call | solution.py:176
  4.9 4.0 %collective-permute-start.4 = (bf16[96,512]{1,0:T(8,128)(2,1)S(1)}, bf16[96,512]{1,0:T(8,128)(2,1)S(1)}, u32[]{:S(2)}, u32[]{:S(2)}) collective-permute-start(bf16[96,512]{1,0:T(8,128)(2,1)S(1)} %get-tuple-element.20), channel_id=1, source_target_pairs={{0,3},{1,2},{2,1},{3,0},{4,7},{5,6},{6,5},{7,4},{8,11},{9,10},{10,... | collective-permute-start | bytes 294920 | tf_op jit(solution)/shard_map/ppermute | solution.py:203
  9.0 0.4 %collective-permute-start.5 = (bf16[96,512]{1,0:T(8,128)(2,1)S(1)}, bf16[96,512]{1,0:T(8,128)(2,1)S(1)}, u32[]{:S(2)}, u32[]{:S(2)}) collective-permute-start(bf16[96,512]{1,0:T(8,128)(2,1)S(1)} %get-tuple-element.21), channel_id=1, source_target_pairs={{0,2},{1,3},{2,0},{3,1},{4,6},{5,7},{6,4},{7,5},{8,10},{9,11},{10,... | collective-permute-start | bytes 294920 | tf_op jit(solution)/shard_map/ppermute | solution.py:203
  9.4 0.2 collective-permute-start.6
  10.3 0.0 copy-done
  10.3 1.3 %collective-permute-start.3 = (bf16[96,384]{1,0:T(8,128)(2,1)S(1)}, bf16[96,384]{1,0:T(8,128)(2,1)S(1)}, u32[]{:S(2)}, u32[]{:S(2)}) collective-permute-start(bf16[96,384]{1,0:T(8,128)(2,1)S(1)} %fusion.otm_ref), channel_id=1, source_target_pairs={{1,0},{2,1},{3,2},{4,3},{5,4},{6,5},{7,6},{9,8},{10,9},{11,10},{12... | collective-permute-start | bytes 221192 | tf_op jit(solution)/shard_map/ppermute | solution.py:206
  11.6 4.0 %collective-permute-start = (bf16[96,512]{1,0:T(8,128)(2,1)S(1)}, bf16[96,512]{1,0:T(8,128)(2,1)S(1)}, u32[]{:S(2)}, u32[]{:S(2)}) collective-permute-start(bf16[96,512]{1,0:T(8,128)(2,1)S(1)} %get-tuple-element.15), channel_id=1, source_target_pairs={{0,3},{1,2},{2,1},{3,0},{4,7},{5,6},{6,5},{7,4},{8,11},{9,10},{10,... | collective-permute-start | bytes 294920 | tf_op jit(solution)/shard_map/ppermute | solution.py:203
  15.6 0.0 collective-permute-done.4
  15.7 0.1 collective-permute-start.1
  15.8 0.0 collective-permute-done.5
  15.8 1.3 %collective-permute-start.2 = (bf16[96,512]{1,0:T(8,128)(2,1)S(1)}, bf16[96,512]{1,0:T(8,128)(2,1)S(1)}, u32[]{:S(2)}, u32[]{:S(2)}) collective-permute-start(bf16[96,512]{1,0:T(8,128)(2,1)S(1)} %get-tuple-element.17), channel_id=1, source_target_pairs={{0,1},{1,0},{2,3},{3,2},{4,5},{5,4},{6,7},{7,6},{8,9},{9,8},{10,11... | collective-permute-start | bytes 294920 | tf_op jit(solution)/shard_map/ppermute | solution.py:203
  17.1 0.0 collective-permute-done.6
  17.1 0.1 add_convert_fusion.1
  17.2 3.0 %collective-permute-start.7 = (bf16[96,512]{1,0:T(8,128)(2,1)S(1)}, bf16[96,512]{1,0:T(8,128)(2,1)S(1)}, u32[]{:S(2)}, u32[]{:S(2)}) collective-permute-start(bf16[96,512]{1,0:T(8,128)(2,1)S(1)} %add_convert_fusion.1), channel_id=1, source_target_pairs={{0,4},{1,5},{2,6},{3,7},{4,0},{5,1},{6,2},{7,3},{8,12},{9,13},{10,... | collective-permute-start | bytes 294920 | tf_op jit(solution)/shard_map/ppermute | solution.py:203
  20.2 0.0 collective-permute-done
  20.2 1.8 %collective-permute-done.1 = bf16[96,512]{1,0:T(8,128)(2,1)S(1)} collective-permute-done((bf16[96,512]{1,0:T(8,128)(2,1)S(1)}, bf16[96,512]{1,0:T(8,128)(2,1)S(1)}, u32[]{:S(2)}, u32[]{:S(2)}) %collective-permute-start.1) | collective-permute-done | bytes 98336 | tf_op jit(solution)/shard_map/ppermute | solution.py:203
  22.0 0.0 collective-permute-done.2
  22.1 0.1 convert_add_fusion
  22.1 0.0 collective-permute-done.3.otm_ref
  22.1 1.3 %collective-permute-done.7 = bf16[96,512]{1,0:T(8,128)(2,1)S(1)} collective-permute-done((bf16[96,512]{1,0:T(8,128)(2,1)S(1)}, bf16[96,512]{1,0:T(8,128)(2,1)S(1)}, u32[]{:S(2)}, u32[]{:S(2)}) %collective-permute-start.7) | collective-permute-done | bytes 98336 | tf_op jit(solution)/shard_map/ppermute | solution.py:203
  23.4 1.3 %collective-permute-start.8 = (bf16[96,512]{1,0:T(8,128)(2,1)S(1)}, bf16[96,512]{1,0:T(8,128)(2,1)S(1)}, u32[]{:S(2)}, u32[]{:S(2)}) collective-permute-start(bf16[96,512]{1,0:T(8,128)(2,1)S(1)} %add_convert_fusion.picked_ref), channel_id=1, source_target_pairs={{1,0},{2,1},{3,2},{4,3},{5,4},{6,5},{7,6},{9,8},{10,9},{11,10},{12... | collective-permute-start | bytes 294920 | tf_op jit(solution)/shard_map/ppermute | solution.py:206
  24.7 2.0 %auto_csd.1 = (bf16[1,4,2,384,384]{4,3,2,1,0:T(8,128)(2,1)}, bf16[128,512]{1,0:T(8,128)(2,1)S(1)}) custom-call(bf16[96,384]{1,0:T(8,128)(2,1)S(1)} %fusion.otm_ref, bf16[96,512]{1,0:T(8,128)(2,1)S(1)} %add_convert_fusion.picked_ref), custom_call_target="tpu_custom_call" | custom-call | tf_op jit(solution)/shard_map/auto_csd/pallas_call | solution.py:221
  26.8 3.2 %collective-permute-done.8.picked_ref = bf16[96,512]{1,0:T(8,128)(2,1)S(1)} collective-permute-done((bf16[96,512]{1,0:T(8,128)(2,1)S(1)}, bf16[96,512]{1,0:T(8,128)(2,1)S(1)}, u32[]{:S(2)}, u32[]{:S(2)}) %collective-permute-start.8) | collective-permute-done | bytes 98336 | tf_op jit(solution)/shard_map/ppermute | solution.py:206
  29.9 1.4 %joint_csd.1 = bf16[1,4,2,128,384]{4,3,2,1,0:T(8,128)(2,1)} custom-call(bf16[128,512]{1,0:T(8,128)(2,1)S(1)} %get-tuple-element.24.left_ref, bf16[96,384]{1,0:T(8,128)(2,1)S(1)} %collective-permute-done.3.otm_ref, bf16[96,512]{1,0:T(8,128)(2,1)S(1)} %collective-permute-done.8.picked_ref), custom_call_target="tpu_custom_call" | custom-call | tf_op jit(solution)/shard_map/joint_csd/pallas_call | solution.py:236
  (3 shorter events, 0.0 us)
Async XLA Ops:
  0.6 9.7 %copy-start = (bf16[1,384,96]{1,2,0:T(8,128)(2,1)S(1)}, bf16[1,384,96]{1,2,0:T(8,128)(2,1)}, u32[]{:S(2)}) copy-start(bf16[1,384,96]{1,2,0:T(8,128)(2,1)} %param.15) | copy-start | bytes 221188
  4.9 10.7 %collective-permute-start.4 = (bf16[96,512]{1,0:T(8,128)(2,1)S(1)}, bf16[96,512]{1,0:T(8,128)(2,1)S(1)}, u32[]{:S(2)}, u32[]{:S(2)}) collective-permute-start(bf16[96,512]{1,0:T(8,128)(2,1)S(1)} %get-tuple-element.20), channel_id=1, source_target_pairs={{0,3},{1,2},{2,1},{3,0},{4,7},{5,6},{6,5},{7,4},{8,11},{9,10},{10,... | collective-permute-start | bytes 294920 | tf_op jit(solution)/shard_map/ppermute | solution.py:203
  9.0 6.8 %collective-permute-start.5 = (bf16[96,512]{1,0:T(8,128)(2,1)S(1)}, bf16[96,512]{1,0:T(8,128)(2,1)S(1)}, u32[]{:S(2)}, u32[]{:S(2)}) collective-permute-start(bf16[96,512]{1,0:T(8,128)(2,1)S(1)} %get-tuple-element.21), channel_id=1, source_target_pairs={{0,2},{1,3},{2,0},{3,1},{4,6},{5,7},{6,4},{7,5},{8,10},{9,11},{10,... | collective-permute-start | bytes 294920 | tf_op jit(solution)/shard_map/ppermute | solution.py:203
  9.4 7.7 %collective-permute-start.6 = (bf16[96,512]{1,0:T(8,128)(2,1)S(1)}, bf16[96,512]{1,0:T(8,128)(2,1)S(1)}, u32[]{:S(2)}, u32[]{:S(2)}) collective-permute-start(bf16[96,512]{1,0:T(8,128)(2,1)S(1)} %get-tuple-element.22), channel_id=1, source_target_pairs={{0,1},{1,0},{2,3},{3,2},{4,5},{5,4},{6,7},{7,6},{8,9},{9,8},{10,11... | collective-permute-start | bytes 294920 | tf_op jit(solution)/shard_map/ppermute | solution.py:203
  10.3 11.8 %collective-permute-start.3 = (bf16[96,384]{1,0:T(8,128)(2,1)S(1)}, bf16[96,384]{1,0:T(8,128)(2,1)S(1)}, u32[]{:S(2)}, u32[]{:S(2)}) collective-permute-start(bf16[96,384]{1,0:T(8,128)(2,1)S(1)} %fusion.otm_ref), channel_id=1, source_target_pairs={{1,0},{2,1},{3,2},{4,3},{5,4},{6,5},{7,6},{9,8},{10,9},{11,10},{12... | collective-permute-start | bytes 221192 | tf_op jit(solution)/shard_map/ppermute | solution.py:206
  11.6 8.6 %collective-permute-start = (bf16[96,512]{1,0:T(8,128)(2,1)S(1)}, bf16[96,512]{1,0:T(8,128)(2,1)S(1)}, u32[]{:S(2)}, u32[]{:S(2)}) collective-permute-start(bf16[96,512]{1,0:T(8,128)(2,1)S(1)} %get-tuple-element.15), channel_id=1, source_target_pairs={{0,3},{1,2},{2,1},{3,0},{4,7},{5,6},{6,5},{7,4},{8,11},{9,10},{10,... | collective-permute-start | bytes 294920 | tf_op jit(solution)/shard_map/ppermute | solution.py:203
  15.7 6.4 %collective-permute-start.1 = (bf16[96,512]{1,0:T(8,128)(2,1)S(1)}, bf16[96,512]{1,0:T(8,128)(2,1)S(1)}, u32[]{:S(2)}, u32[]{:S(2)}) collective-permute-start(bf16[96,512]{1,0:T(8,128)(2,1)S(1)} %get-tuple-element.16), channel_id=1, source_target_pairs={{0,2},{1,3},{2,0},{3,1},{4,6},{5,7},{6,4},{7,5},{8,10},{9,11},{10,... | collective-permute-start | bytes 294920 | tf_op jit(solution)/shard_map/ppermute | solution.py:203
  15.8 6.3 %collective-permute-start.2 = (bf16[96,512]{1,0:T(8,128)(2,1)S(1)}, bf16[96,512]{1,0:T(8,128)(2,1)S(1)}, u32[]{:S(2)}, u32[]{:S(2)}) collective-permute-start(bf16[96,512]{1,0:T(8,128)(2,1)S(1)} %get-tuple-element.17), channel_id=1, source_target_pairs={{0,1},{1,0},{2,3},{3,2},{4,5},{5,4},{6,7},{7,6},{8,9},{9,8},{10,11... | collective-permute-start | bytes 294920 | tf_op jit(solution)/shard_map/ppermute | solution.py:203
  17.2 6.2 %collective-permute-start.7 = (bf16[96,512]{1,0:T(8,128)(2,1)S(1)}, bf16[96,512]{1,0:T(8,128)(2,1)S(1)}, u32[]{:S(2)}, u32[]{:S(2)}) collective-permute-start(bf16[96,512]{1,0:T(8,128)(2,1)S(1)} %add_convert_fusion.1), channel_id=1, source_target_pairs={{0,4},{1,5},{2,6},{3,7},{4,0},{5,1},{6,2},{7,3},{8,12},{9,13},{10,... | collective-permute-start | bytes 294920 | tf_op jit(solution)/shard_map/ppermute | solution.py:203
  23.4 6.5 %collective-permute-start.8 = (bf16[96,512]{1,0:T(8,128)(2,1)S(1)}, bf16[96,512]{1,0:T(8,128)(2,1)S(1)}, u32[]{:S(2)}, u32[]{:S(2)}) collective-permute-start(bf16[96,512]{1,0:T(8,128)(2,1)S(1)} %add_convert_fusion.picked_ref), channel_id=1, source_target_pairs={{1,0},{2,1},{3,2},{4,3},{5,4},{6,5},{7,6},{9,8},{10,9},{11,10},{12... | collective-permute-start | bytes 294920 | tf_op jit(solution)/shard_map/ppermute | solution.py:206

commit v4 on v3

--- a/solution.py
+++ b/solution.py
@@ -140,11 +140,14 @@
         copy.wait()
 
 
-def joint_kernel(left_ref, otm_ref, picked_ref, joint_hbm, buffer, sems):
+def joint_kernel(left_ref, joined_ref, joint_hbm, buffer, sems):
     lines = buffer.shape[0]
-    z = lax.dot_general(otm_ref[...], picked_ref[...], TN, preferred_element_type=F32)
+    columns = left_ref.shape[1]
+    z = lax.dot_general(
+        joined_ref[:, columns:], joined_ref[:, :columns], TN, preferred_element_type=F32
+    )
     z = z.astype(BF16)
-    pair = z.shape[1] // lines
+    pair = columns // lines
     copies = []
     for f in range(lines):
         columns = slice(f * pair, (f + 1) * pair)
@@ -208,14 +211,13 @@
     far_sum = far_own
     for k, value in zip(steps, far):
         far_sum = far_sum + swapped(value, k).astype(F32)
-    next_otm = following(own_otm)
     picked = near_own
     for k, value in zip(steps, near):
         picked = picked + swapped(value, k).astype(F32)
-    across = swapped(far_sum.astype(BF16), half)
-    picked, next_otm = lax.optimization_barrier((picked, next_otm))
-    picked = (picked + across.astype(F32)).astype(BF16)
-    next_picked = following(picked)
+    far_sum, own_otm = lax.optimization_barrier((far_sum.astype(BF16), own_otm))
+    picked = picked + swapped(far_sum, half).astype(F32)
+    picked = picked.astype(BF16)
+    joined = following(jnp.concatenate([picked, own_otm], axis=1))
 
     params = pltpu.CompilerParams(vmem_limit_bytes=24 << 20)
     csd, left = pl.pallas_call(
@@ -236,7 +238,7 @@
     joint = pl.pallas_call(
         joint_kernel,
         out_shape=jax.ShapeDtypeStruct((1, lines, 2, CROSS, rows_max), BF16),
-        in_specs=[vmem] * 3,
+        in_specs=[vmem] * 2,
         out_specs=hbm,
         scratch_shapes=[
             pltpu.VMEM((lines, 2, CROSS, rows_max), BF16),
@@ -244,7 +246,7 @@
         ],
         compiler_params=params,
         name="joint_csd",
-    )(left, next_otm, next_picked)
+    )(left, joined)
     return (csd, joint)
 
 

time: 31.5 us -> 30.9 us (0.981)
  starting transfers between devices: 15.8 us -> 12.9 us
  waiting for transfers between devices: 6.31 us -> 8.61 us
    ppermute x7, starting transfers between devices: 13.2 us -> 11.6 us  [swapped(): return lax.ppermute(value, 'mode', [(i, i ^ k) for i in range(count)])]
    ppermute x7, waiting for transfers between devices: 3.13 us -> 4.64 us  [swapped(): return lax.ppermute(value, 'mode', [(i, i ^ k) for i in range(count)])]
    ppermute x2 -> x1, starting transfers between devices: 2.58 us -> 1.29 us  [following(): return lax.ppermute(value, 'mode', [(i, i - 1) for i in range(1, count)])]
    ppermute x2 -> x1, waiting for transfers between devices: 3.18 us -> 3.97 us  [following(): return lax.ppermute(value, 'mode', [(i, i - 1) for i in range(1, count)])]
  transfers between devices with their start and end apart: 9 -> 8, of which waited for: 3 -> 5; matrix products, arithmetic and copies ran while one was open for 0% -> 0% of each run, Pallas kernels for 6% -> 7%
where the time goes in v4:
time: 30.9 us; the launch traced here: 30.7 us
  starting transfers between devices  12.9 us (42%)
  waiting for transfers between devices  8.61 us (28%)
  Pallas kernels  7.66 us (25%)
  between operations  1.37 us (4%)
    ppermute x7, starting transfers between devices, swapped(): return lax.ppermute(value, 'mode', [(i, i ^ k) for i in range(count)])  11.6 us
    ppermute x7, waiting for transfers between devices, swapped(): return lax.ppermute(value, 'mode', [(i, i ^ k) for i in range(count)])  4.64 us
    pallas_call x1, Pallas kernels, per_device(): pl.pallas_call(functools.partial(parts_kernel, slots), out_shape=([part]...  4.28 us
    ppermute x1, waiting for transfers between devices, following(): return lax.ppermute(value, 'mode', [(i, i - 1) for i in range(1, count)])  3.97 us
    pallas_call x1, Pallas kernels, per_device(): pl.pallas_call(auto_kernel, out_shape=[jax.ShapeDtypeStruct((1, lines, 2,...  2.02 us
    pallas_call x1, Pallas kernels, per_device(): pl.pallas_call(joint_kernel, out_shape=jax.ShapeDtypeStruct((1, lines, 2,...  1.36 us
    ppermute x1, starting transfers between devices, following(): return lax.ppermute(value, 'mode', [(i, i - 1) for i in range(1, count)])  1.29 us
  transfers between devices with their start and end apart: 8, of which 5 were waited for; matrix products, arithmetic and copies ran while one was open for 0% of the time, Pallas kernels for 7%

profile of v4, /device:TPU:0, one launch (start us, length us, event | category | flops | bytes accessed | tf_op | source)
XLA Modules:
  0.0 30.7 jit_solution(6927124405175930203)
XLA Ops:
  0.6 0.0 copy-start
  0.6 4.3 %partial_sums.1 = (bf16[96,512]{1,0:T(8,128)(2,1)S(1)}, bf16[96,512]{1,0:T(8,128)(2,1)S(1)}, bf16[96,512]{1,0:T(8,128)(2,1)S(1)}, f32[96,512]{1,0:T(8,128)S(1)},...) custom-call(s32[8,96]{1,0:T(8,128)} %attach_hbm.1, ...), custom_call_target="tpu_custom_call" | custom-call | tf_op jit(solution)/shard_map/partial_sums/pallas_call | solution.py:179
  4.9 4.0 %collective-permute-start = (bf16[96,512]{1,0:T(8,128)(2,1)S(1)}, bf16[96,512]{1,0:T(8,128)(2,1)S(1)}, u32[]{:S(2)}, u32[]{:S(2)}) collective-permute-start(bf16[96,512]{1,0:T(8,128)(2,1)S(1)} %get-tuple-element.15), channel_id=1, source_target_pairs={{0,3},{1,2},{2,1},{3,0},{4,7},{5,6},{6,5},{7,4},{8,11},{9,10},{10,... | collective-permute-start | bytes 294920 | tf_op jit(solution)/shard_map/ppermute | solution.py:206
  9.0 0.5 %collective-permute-start.1 = (bf16[96,512]{1,0:T(8,128)(2,1)S(1)}, bf16[96,512]{1,0:T(8,128)(2,1)S(1)}, u32[]{:S(2)}, u32[]{:S(2)}) collective-permute-start(bf16[96,512]{1,0:T(8,128)(2,1)S(1)} %get-tuple-element.16), channel_id=1, source_target_pairs={{0,2},{1,3},{2,0},{3,1},{4,6},{5,7},{6,4},{7,5},{8,10},{9,11},{10,... | collective-permute-start | bytes 294920 | tf_op jit(solution)/shard_map/ppermute | solution.py:206
  9.4 0.2 collective-permute-start.2
  9.6 2.8 %collective-permute-start.3 = (bf16[96,512]{1,0:T(8,128)(2,1)S(1)}, bf16[96,512]{1,0:T(8,128)(2,1)S(1)}, u32[]{:S(2)}, u32[]{:S(2)}) collective-permute-start(bf16[96,512]{1,0:T(8,128)(2,1)S(1)} %get-tuple-element.20), channel_id=1, source_target_pairs={{0,3},{1,2},{2,1},{3,0},{4,7},{5,6},{6,5},{7,4},{8,11},{9,10},{10,... | collective-permute-start | bytes 294920 | tf_op jit(solution)/shard_map/ppermute | solution.py:206
  12.5 0.5 %collective-permute-start.4 = (bf16[96,512]{1,0:T(8,128)(2,1)S(1)}, bf16[96,512]{1,0:T(8,128)(2,1)S(1)}, u32[]{:S(2)}, u32[]{:S(2)}) collective-permute-start(bf16[96,512]{1,0:T(8,128)(2,1)S(1)} %get-tuple-element.21), channel_id=1, source_target_pairs={{0,2},{1,3},{2,0},{3,1},{4,6},{5,7},{6,4},{7,5},{8,10},{9,11},{10,... | collective-permute-start | bytes 294920 | tf_op jit(solution)/shard_map/ppermute | solution.py:206
  13.6 0.0 copy-done
  13.6 0.0 collective-permute-done
  13.6 0.8 %collective-permute-start.5 = (bf16[96,512]{1,0:T(8,128)(2,1)S(1)}, bf16[96,512]{1,0:T(8,128)(2,1)S(1)}, u32[]{:S(2)}, u32[]{:S(2)}) collective-permute-start(bf16[96,512]{1,0:T(8,128)(2,1)S(1)} %get-tuple-element.22), channel_id=1, source_target_pairs={{0,1},{1,0},{2,3},{3,2},{4,5},{5,4},{6,7},{7,6},{8,9},{9,8},{10,11... | collective-permute-start | bytes 294920 | tf_op jit(solution)/shard_map/ppermute | solution.py:206
  14.4 0.6 %collective-permute-done.1 = bf16[96,512]{1,0:T(8,128)(2,1)S(1)} collective-permute-done((bf16[96,512]{1,0:T(8,128)(2,1)S(1)}, bf16[96,512]{1,0:T(8,128)(2,1)S(1)}, u32[]{:S(2)}, u32[]{:S(2)}) %collective-permute-start.1) | collective-permute-done | bytes 98336 | tf_op jit(solution)/shard_map/ppermute | solution.py:206
  15.0 0.6 %collective-permute-done.2 = bf16[96,512]{1,0:T(8,128)(2,1)S(1)} collective-permute-done((bf16[96,512]{1,0:T(8,128)(2,1)S(1)}, bf16[96,512]{1,0:T(8,128)(2,1)S(1)}, u32[]{:S(2)}, u32[]{:S(2)}) %collective-permute-start.2) | collective-permute-done | bytes 98336 | tf_op jit(solution)/shard_map/ppermute | solution.py:206
  15.6 0.1 add_convert_fusion.1
  15.7 2.9 %collective-permute-start.6 = (bf16[96,512]{1,0:T(8,128)(2,1)S(1)}, bf16[96,512]{1,0:T(8,128)(2,1)S(1)}, u32[]{:S(2)}, u32[]{:S(2)}) collective-permute-start(bf16[96,512]{1,0:T(8,128)(2,1)S(1)} %add_convert_fusion.1), channel_id=1, source_target_pairs={{0,4},{1,5},{2,6},{3,7},{4,0},{5,1},{6,2},{7,3},{8,12},{9,13},{10,... | collective-permute-start | bytes 294920 | tf_op jit(solution)/shard_map/ppermute | solution.py:206
  18.5 0.0 collective-permute-done.3
  18.5 0.8 %collective-permute-done.4 = bf16[96,512]{1,0:T(8,128)(2,1)S(1)} collective-permute-done((bf16[96,512]{1,0:T(8,128)(2,1)S(1)}, bf16[96,512]{1,0:T(8,128)(2,1)S(1)}, u32[]{:S(2)}, u32[]{:S(2)}) %collective-permute-start.4) | collective-permute-done | bytes 98336 | tf_op jit(solution)/shard_map/ppermute | solution.py:206
  19.4 0.0 collective-permute-done.5
  19.4 2.5 %collective-permute-done.6 = bf16[96,512]{1,0:T(8,128)(2,1)S(1)} collective-permute-done((bf16[96,512]{1,0:T(8,128)(2,1)S(1)}, bf16[96,512]{1,0:T(8,128)(2,1)S(1)}, u32[]{:S(2)}, u32[]{:S(2)}) %collective-permute-start.6) | collective-permute-done | bytes 98336 | tf_op jit(solution)/shard_map/ppermute | solution.py:206
  21.9 0.1 add_convert_fusion.picked_ref
  22.0 1.3 %collective-permute-start.7 = (bf16[96,896]{1,0:T(8,128)(2,1)S(1)}, bf16[96,896]{1,0:T(8,128)(2,1)S(1)}, u32[]{:S(2)}, u32[]{:S(2)}) collective-permute-start(bf16[96,896]{1,0:T(8,128)(2,1)S(1)} %pad_maximum_fusion), channel_id=1, source_target_pairs={{1,0},{2,1},{3,2},{4,3},{5,4},{6,5},{7,6},{9,8},{10,9},{11,10},{12... | collective-permute-start | bytes 516104 | tf_op jit(solution)/shard_map/ppermute | solution.py:209
  23.3 2.0 %auto_csd.1 = (bf16[1,4,2,384,384]{4,3,2,1,0:T(8,128)(2,1)}, bf16[128,512]{1,0:T(8,128)(2,1)S(1)}) custom-call(bf16[96,384]{1,0:T(8,128)(2,1)S(1)} %fusion.otm_ref, bf16[96,512]{1,0:T(8,128)(2,1)S(1)} %add_convert_fusion.picked_ref), custom_call_target="tpu_custom_call" | custom-call | tf_op jit(solution)/shard_map/auto_csd/pallas_call | solution.py:223
  25.4 4.0 %collective-permute-done.7.joined_ref = bf16[96,896]{1,0:T(8,128)(2,1)S(1)} collective-permute-done((bf16[96,896]{1,0:T(8,128)(2,1)S(1)}, bf16[96,896]{1,0:T(8,128)(2,1)S(1)}, u32[]{:S(2)}, u32[]{:S(2)}) %collective-permute-start.7) | collective-permute-done | bytes 172064 | tf_op jit(solution)/shard_map/ppermute | solution.py:209
  29.3 1.4 %joint_csd.1 = bf16[1,4,2,128,384]{4,3,2,1,0:T(8,128)(2,1)} custom-call(bf16[128,512]{1,0:T(8,128)(2,1)S(1)} %get-tuple-element.25.left_ref, bf16[96,896]{1,0:T(8,128)(2,1)S(1)} %collective-permute-done.7.joined_ref), custom_call_target="tpu_custom_call" | custom-call | tf_op jit(solution)/shard_map/joint_csd/pallas_call | solution.py:238
  (3 shorter events, 0.0 us)
Async XLA Ops:
  0.6 12.9 %copy-start = (bf16[1,384,96]{1,2,0:T(8,128)(2,1)S(1)}, bf16[1,384,96]{1,2,0:T(8,128)(2,1)}, u32[]{:S(2)}) copy-start(bf16[1,384,96]{1,2,0:T(8,128)(2,1)} %param.15) | copy-start | bytes 221188
  4.9 8.7 %collective-permute-start = (bf16[96,512]{1,0:T(8,128)(2,1)S(1)}, bf16[96,512]{1,0:T(8,128)(2,1)S(1)}, u32[]{:S(2)}, u32[]{:S(2)}) collective-permute-start(bf16[96,512]{1,0:T(8,128)(2,1)S(1)} %get-tuple-element.15), channel_id=1, source_target_pairs={{0,3},{1,2},{2,1},{3,0},{4,7},{5,6},{6,5},{7,4},{8,11},{9,10},{10,... | collective-permute-start | bytes 294920 | tf_op jit(solution)/shard_map/ppermute | solution.py:206
  9.0 6.0 %collective-permute-start.1 = (bf16[96,512]{1,0:T(8,128)(2,1)S(1)}, bf16[96,512]{1,0:T(8,128)(2,1)S(1)}, u32[]{:S(2)}, u32[]{:S(2)}) collective-permute-start(bf16[96,512]{1,0:T(8,128)(2,1)S(1)} %get-tuple-element.16), channel_id=1, source_target_pairs={{0,2},{1,3},{2,0},{3,1},{4,6},{5,7},{6,4},{7,5},{8,10},{9,11},{10,... | collective-permute-start | bytes 294920 | tf_op jit(solution)/shard_map/ppermute | solution.py:206
  9.4 6.2 %collective-permute-start.2 = (bf16[96,512]{1,0:T(8,128)(2,1)S(1)}, bf16[96,512]{1,0:T(8,128)(2,1)S(1)}, u32[]{:S(2)}, u32[]{:S(2)}) collective-permute-start(bf16[96,512]{1,0:T(8,128)(2,1)S(1)} %get-tuple-element.17), channel_id=1, source_target_pairs={{0,1},{1,0},{2,3},{3,2},{4,5},{5,4},{6,7},{7,6},{8,9},{9,8},{10,11... | collective-permute-start | bytes 294920 | tf_op jit(solution)/shard_map/ppermute | solution.py:206
  9.6 8.9 %collective-permute-start.3 = (bf16[96,512]{1,0:T(8,128)(2,1)S(1)}, bf16[96,512]{1,0:T(8,128)(2,1)S(1)}, u32[]{:S(2)}, u32[]{:S(2)}) collective-permute-start(bf16[96,512]{1,0:T(8,128)(2,1)S(1)} %get-tuple-element.20), channel_id=1, source_target_pairs={{0,3},{1,2},{2,1},{3,0},{4,7},{5,6},{6,5},{7,4},{8,11},{9,10},{10,... | collective-permute-start | bytes 294920 | tf_op jit(solution)/shard_map/ppermute | solution.py:206
  12.5 6.9 %collective-permute-start.4 = (bf16[96,512]{1,0:T(8,128)(2,1)S(1)}, bf16[96,512]{1,0:T(8,128)(2,1)S(1)}, u32[]{:S(2)}, u32[]{:S(2)}) collective-permute-start(bf16[96,512]{1,0:T(8,128)(2,1)S(1)} %get-tuple-element.21), channel_id=1, source_target_pairs={{0,2},{1,3},{2,0},{3,1},{4,6},{5,7},{6,4},{7,5},{8,10},{9,11},{10,... | collective-permute-start | bytes 294920 | tf_op jit(solution)/shard_map/ppermute | solution.py:206
  13.6 5.8 %collective-permute-start.5 = (bf16[96,512]{1,0:T(8,128)(2,1)S(1)}, bf16[96,512]{1,0:T(8,128)(2,1)S(1)}, u32[]{:S(2)}, u32[]{:S(2)}) collective-permute-start(bf16[96,512]{1,0:T(8,128)(2,1)S(1)} %get-tuple-element.22), channel_id=1, source_target_pairs={{0,1},{1,0},{2,3},{3,2},{4,5},{5,4},{6,7},{7,6},{8,9},{9,8},{10,11... | collective-permute-start | bytes 294920 | tf_op jit(solution)/shard_map/ppermute | solution.py:206
  15.7 6.3 %collective-permute-start.6 = (bf16[96,512]{1,0:T(8,128)(2,1)S(1)}, bf16[96,512]{1,0:T(8,128)(2,1)S(1)}, u32[]{:S(2)}, u32[]{:S(2)}) collective-permute-start(bf16[96,512]{1,0:T(8,128)(2,1)S(1)} %add_convert_fusion.1), channel_id=1, source_target_pairs={{0,4},{1,5},{2,6},{3,7},{4,0},{5,1},{6,2},{7,3},{8,12},{9,13},{10,... | collective-permute-start | bytes 294920 | tf_op jit(solution)/shard_map/ppermute | solution.py:206
  22.0 7.3 %collective-permute-start.7 = (bf16[96,896]{1,0:T(8,128)(2,1)S(1)}, bf16[96,896]{1,0:T(8,128)(2,1)S(1)}, u32[]{:S(2)}, u32[]{:S(2)}) collective-permute-start(bf16[96,896]{1,0:T(8,128)(2,1)S(1)} %pad_maximum_fusion), channel_id=1, source_target_pairs={{1,0},{2,1},{3,2},{4,3},{5,4},{6,5},{7,6},{9,8},{10,9},{11,10},{12... | collective-permute-start | bytes 516104 | tf_op jit(solution)/shard_map/ppermute | solution.py:209

commit v5 on v4

--- a/solution.py
+++ b/solution.py
@@ -8,11 +8,12 @@
 from jax.sharding import PartitionSpec as P
 
 CROSS = 128
-CHUNKS = 6
+CHUNKS = 4
 LANES = 128
 F32 = jnp.float32
 BF16 = jnp.bfloat16
 NT = (((1,), (1,)), ((), ()))
+NN = (((1,), (0,)), ((), ()))
 TN = (((0,), (0,)), ((), ()))
 
 
@@ -67,7 +68,7 @@
         return pltpu.make_async_copy(shapes_hbm.at[rows, :], raw.at[rows, :], sems.at[i])
 
     for i in range(chunks):
-        fetch(i).start()
+        fetch(i).start(priority=i % 2)
     for copy in copies:
         copy.wait()
     modal_response(freq, damp, exc, load, resp)
@@ -89,11 +90,13 @@
         for a in range(att):
             picks[pl.ds(first + a * pieces, pieces), :] = rows[a]
 
-    for i, slot in enumerate(slots):
+    group = min(4, len(slots))
+    for i, slot in enumerate(slots[:group]):
         pick(slot, i * att * pieces)
-    group = min(8, len(slots))
     for start in range(0, len(slots), group):
         count = group * att
+        for i, slot in enumerate(slots[start + group : start + 2 * group]):
+            pick(slot, (start + group + i) * att * pieces)
         lhs = jnp.concatenate(
             [
                 picks[pl.ds(start * att * pieces + k, count, stride=pieces), :].astype(BF16)
@@ -112,11 +115,10 @@
     return jnp.concatenate([z[:, width:], -z[:, :width]], axis=1)
 
 
-def spectra(left, right, out_hbm, buffer, sems, f):
-    pair = left.shape[1]
-    rows = left.shape[0]
-    both = jnp.concatenate([left, turned(left)], axis=0)
-    value = lax.dot_general(both, right, NT, preferred_element_type=F32) * (2.0 / pair)
+def spectra(both, right, out_hbm, buffer, sems, f, form=NT):
+    pair = both.shape[1]
+    rows = both.shape[0] // 2
+    value = lax.dot_general(both, right, form, preferred_element_type=F32) * (2.0 / pair)
     value = value.astype(BF16)
     buffer[f, 0] = value[:rows]
     buffer[f, 1] = value[rows:]
@@ -127,15 +129,16 @@
 
 def auto_kernel(otm_ref, picked_ref, csd_hbm, left_ref, buffer, sems):
     lines = buffer.shape[0]
-    cross = left_ref.shape[0]
+    cross = left_ref.shape[0] // 2
     z = lax.dot_general(otm_ref[...], picked_ref[...], TN, preferred_element_type=F32)
     z = z.astype(BF16)
     pair = z.shape[1] // lines
-    left_ref[...] = z[:cross]
     copies = []
     for f in range(lines):
         line = z[:, f * pair : (f + 1) * pair]
-        copies.append(spectra(line, line, csd_hbm, buffer, sems, f))
+        left_ref[: cross, f * pair : (f + 1) * pair] = line[:cross]
+        left_ref[cross :, f * pair : (f + 1) * pair] = turned(line[:cross])
+        copies.append(spectra(jnp.concatenate([line, turned(line)], axis=0), line, csd_hbm, buffer, sems, f))
     for copy in copies:
         copy.wait()
 
@@ -144,15 +147,15 @@
     lines = buffer.shape[0]
     columns = left_ref.shape[1]
     z = lax.dot_general(
-        joined_ref[:, columns:], joined_ref[:, :columns], TN, preferred_element_type=F32
+        joined_ref[:, :columns], joined_ref[:, columns:], TN, preferred_element_type=F32
     )
     z = z.astype(BF16)
     pair = columns // lines
     copies = []
     for f in range(lines):
-        columns = slice(f * pair, (f + 1) * pair)
+        part = slice(f * pair, (f + 1) * pair)
         copies.append(
-            spectra(left_ref[:, columns], z[:, columns], joint_hbm, buffer, sems, f)
+            spectra(left_ref[:, part], z[part], joint_hbm, buffer, sems, f, NN)
         )
     for copy in copies:
         copy.wait()
@@ -224,7 +227,7 @@
         auto_kernel,
         out_shape=[
             jax.ShapeDtypeStruct((1, lines, 2, rows_max, rows_max), BF16),
-            jax.ShapeDtypeStruct((CROSS, columns), BF16),
+            jax.ShapeDtypeStruct((2 * CROSS, columns), BF16),
         ],
         in_specs=[vmem] * 2,
         out_specs=[hbm, vmem],

time: 30.9 us -> 30.7 us (level)
  no operation moved by 1% of the time
where the time goes in v5:
time: 30.7 us; the launch traced here: 30.5 us
  starting transfers between devices  12.9 us (42%)
  waiting for transfers between devices  8.65 us (28%)
  Pallas kernels  7.45 us (24%)
  between operations  1.37 us (4%)
    ppermute x7, starting transfers between devices, swapped(): return lax.ppermute(value, 'mode', [(i, i ^ k) for i in range(count)])  11.6 us
    ppermute x7, waiting for transfers between devices, swapped(): return lax.ppermute(value, 'mode', [(i, i ^ k) for i in range(count)])  4.67 us
    pallas_call x1, Pallas kernels, per_device(): pl.pallas_call(functools.partial(parts_kernel, slots), out_shape=([part]...  4.12 us
    ppermute x1, waiting for transfers between devices, following(): return lax.ppermute(value, 'mode', [(i, i - 1) for i in range(1, count)])  3.97 us
    pallas_call x1, Pallas kernels, per_device(): pl.pallas_call(auto_kernel, out_shape=[jax.ShapeDtypeStruct((1, lines, 2,...  2.02 us
    pallas_call x1, Pallas kernels, per_device(): pl.pallas_call(joint_kernel, out_shape=jax.ShapeDtypeStruct((1, lines, 2,...  1.31 us
    ppermute x1, starting transfers between devices, following(): return lax.ppermute(value, 'mode', [(i, i - 1) for i in range(1, count)])  1.29 us
  transfers between devices with their start and end apart: 8, of which 5 were waited for; matrix products, arithmetic and copies ran while one was open for 0% of the time, Pallas kernels for 7%

profile of v5, /device:TPU:0, one launch (start us, length us, event | category | flops | bytes accessed | tf_op | source)
XLA Modules:
  0.0 30.5 jit_solution(5821683542221009483)
XLA Ops:
  0.6 0.0 copy-start
  0.6 4.1 %partial_sums.1 = (bf16[96,512]{1,0:T(8,128)(2,1)S(1)}, bf16[96,512]{1,0:T(8,128)(2,1)S(1)}, bf16[96,512]{1,0:T(8,128)(2,1)S(1)}, f32[96,512]{1,0:T(8,128)S(1)},...) custom-call(s32[8,96]{1,0:T(8,128)} %attach_hbm.1, ...), custom_call_target="tpu_custom_call" | custom-call | tf_op jit(solution)/shard_map/partial_sums/pallas_call | solution.py:182
  4.8 4.0 %collective-permute-start = (bf16[96,512]{1,0:T(8,128)(2,1)S(1)}, bf16[96,512]{1,0:T(8,128)(2,1)S(1)}, u32[]{:S(2)}, u32[]{:S(2)}) collective-permute-start(bf16[96,512]{1,0:T(8,128)(2,1)S(1)} %get-tuple-element.15), channel_id=1, source_target_pairs={{0,3},{1,2},{2,1},{3,0},{4,7},{5,6},{6,5},{7,4},{8,11},{9,10},{10,... | collective-permute-start | bytes 294920 | tf_op jit(solution)/shard_map/ppermute | solution.py:209
  8.8 0.5 %collective-permute-start.1 = (bf16[96,512]{1,0:T(8,128)(2,1)S(1)}, bf16[96,512]{1,0:T(8,128)(2,1)S(1)}, u32[]{:S(2)}, u32[]{:S(2)}) collective-permute-start(bf16[96,512]{1,0:T(8,128)(2,1)S(1)} %get-tuple-element.16), channel_id=1, source_target_pairs={{0,2},{1,3},{2,0},{3,1},{4,6},{5,7},{6,4},{7,5},{8,10},{9,11},{10,... | collective-permute-start | bytes 294920 | tf_op jit(solution)/shard_map/ppermute | solution.py:209
  9.3 0.2 collective-permute-start.2
  9.5 2.8 %collective-permute-start.3 = (bf16[96,512]{1,0:T(8,128)(2,1)S(1)}, bf16[96,512]{1,0:T(8,128)(2,1)S(1)}, u32[]{:S(2)}, u32[]{:S(2)}) collective-permute-start(bf16[96,512]{1,0:T(8,128)(2,1)S(1)} %get-tuple-element.20), channel_id=1, source_target_pairs={{0,3},{1,2},{2,1},{3,0},{4,7},{5,6},{6,5},{7,4},{8,11},{9,10},{10,... | collective-permute-start | bytes 294920 | tf_op jit(solution)/shard_map/ppermute | solution.py:209
  12.3 0.5 %collective-permute-start.4 = (bf16[96,512]{1,0:T(8,128)(2,1)S(1)}, bf16[96,512]{1,0:T(8,128)(2,1)S(1)}, u32[]{:S(2)}, u32[]{:S(2)}) collective-permute-start(bf16[96,512]{1,0:T(8,128)(2,1)S(1)} %get-tuple-element.21), channel_id=1, source_target_pairs={{0,2},{1,3},{2,0},{3,1},{4,6},{5,7},{6,4},{7,5},{8,10},{9,11},{10,... | collective-permute-start | bytes 294920 | tf_op jit(solution)/shard_map/ppermute | solution.py:209
  13.4 0.0 copy-done
  13.4 0.0 collective-permute-done
  13.5 0.8 %collective-permute-start.5 = (bf16[96,512]{1,0:T(8,128)(2,1)S(1)}, bf16[96,512]{1,0:T(8,128)(2,1)S(1)}, u32[]{:S(2)}, u32[]{:S(2)}) collective-permute-start(bf16[96,512]{1,0:T(8,128)(2,1)S(1)} %get-tuple-element.22), channel_id=1, source_target_pairs={{0,1},{1,0},{2,3},{3,2},{4,5},{5,4},{6,7},{7,6},{8,9},{9,8},{10,11... | collective-permute-start | bytes 294920 | tf_op jit(solution)/shard_map/ppermute | solution.py:209
  14.2 0.6 %collective-permute-done.1 = bf16[96,512]{1,0:T(8,128)(2,1)S(1)} collective-permute-done((bf16[96,512]{1,0:T(8,128)(2,1)S(1)}, bf16[96,512]{1,0:T(8,128)(2,1)S(1)}, u32[]{:S(2)}, u32[]{:S(2)}) %collective-permute-start.1) | collective-permute-done | bytes 98336 | tf_op jit(solution)/shard_map/ppermute | solution.py:209
  14.9 0.6 %collective-permute-done.2 = bf16[96,512]{1,0:T(8,128)(2,1)S(1)} collective-permute-done((bf16[96,512]{1,0:T(8,128)(2,1)S(1)}, bf16[96,512]{1,0:T(8,128)(2,1)S(1)}, u32[]{:S(2)}, u32[]{:S(2)}) %collective-permute-start.2) | collective-permute-done | bytes 98336 | tf_op jit(solution)/shard_map/ppermute | solution.py:209
  15.5 0.1 add_convert_fusion.1
  15.5 2.8 %collective-permute-start.6 = (bf16[96,512]{1,0:T(8,128)(2,1)S(1)}, bf16[96,512]{1,0:T(8,128)(2,1)S(1)}, u32[]{:S(2)}, u32[]{:S(2)}) collective-permute-start(bf16[96,512]{1,0:T(8,128)(2,1)S(1)} %add_convert_fusion.1), channel_id=1, source_target_pairs={{0,4},{1,5},{2,6},{3,7},{4,0},{5,1},{6,2},{7,3},{8,12},{9,13},{10,... | collective-permute-start | bytes 294920 | tf_op jit(solution)/shard_map/ppermute | solution.py:209
  18.4 0.0 collective-permute-done.3
  18.4 0.9 %collective-permute-done.4 = bf16[96,512]{1,0:T(8,128)(2,1)S(1)} collective-permute-done((bf16[96,512]{1,0:T(8,128)(2,1)S(1)}, bf16[96,512]{1,0:T(8,128)(2,1)S(1)}, u32[]{:S(2)}, u32[]{:S(2)}) %collective-permute-start.4) | collective-permute-done | bytes 98336 | tf_op jit(solution)/shard_map/ppermute | solution.py:209
  19.2 0.0 collective-permute-done.5
  19.2 2.6 %collective-permute-done.6 = bf16[96,512]{1,0:T(8,128)(2,1)S(1)} collective-permute-done((bf16[96,512]{1,0:T(8,128)(2,1)S(1)}, bf16[96,512]{1,0:T(8,128)(2,1)S(1)}, u32[]{:S(2)}, u32[]{:S(2)}) %collective-permute-start.6) | collective-permute-done | bytes 98336 | tf_op jit(solution)/shard_map/ppermute | solution.py:209
  21.8 0.1 add_convert_fusion.picked_ref
  21.9 1.3 %collective-permute-start.7 = (bf16[96,896]{1,0:T(8,128)(2,1)S(1)}, bf16[96,896]{1,0:T(8,128)(2,1)S(1)}, u32[]{:S(2)}, u32[]{:S(2)}) collective-permute-start(bf16[96,896]{1,0:T(8,128)(2,1)S(1)} %pad_maximum_fusion), channel_id=1, source_target_pairs={{1,0},{2,1},{3,2},{4,3},{5,4},{6,5},{7,6},{9,8},{10,9},{11,10},{12... | collective-permute-start | bytes 516104 | tf_op jit(solution)/shard_map/ppermute | solution.py:212
  23.2 2.0 %auto_csd.1 = (bf16[1,4,2,384,384]{4,3,2,1,0:T(8,128)(2,1)}, bf16[256,512]{1,0:T(8,128)(2,1)S(1)}) custom-call(bf16[96,384]{1,0:T(8,128)(2,1)S(1)} %fusion.otm_ref, bf16[96,512]{1,0:T(8,128)(2,1)S(1)} %add_convert_fusion.picked_ref), custom_call_target="tpu_custom_call" | custom-call | tf_op jit(solution)/shard_map/auto_csd/pallas_call | solution.py:226
  25.2 4.0 %collective-permute-done.7.joined_ref = bf16[96,896]{1,0:T(8,128)(2,1)S(1)} collective-permute-done((bf16[96,896]{1,0:T(8,128)(2,1)S(1)}, bf16[96,896]{1,0:T(8,128)(2,1)S(1)}, u32[]{:S(2)}, u32[]{:S(2)}) %collective-permute-start.7) | collective-permute-done | bytes 172064 | tf_op jit(solution)/shard_map/ppermute | solution.py:212
  29.2 1.3 %joint_csd.1 = bf16[1,4,2,128,384]{4,3,2,1,0:T(8,128)(2,1)} custom-call(bf16[256,512]{1,0:T(8,128)(2,1)S(1)} %get-tuple-element.25.left_ref, bf16[96,896]{1,0:T(8,128)(2,1)S(1)} %collective-permute-done.7.joined_ref), custom_call_target="tpu_custom_call" | custom-call | tf_op jit(solution)/shard_map/joint_csd/pallas_call | solution.py:241
  (3 shorter events, 0.0 us)
Async XLA Ops:
  0.6 12.8 %copy-start = (bf16[1,384,96]{1,2,0:T(8,128)(2,1)S(1)}, bf16[1,384,96]{1,2,0:T(8,128)(2,1)}, u32[]{:S(2)}) copy-start(bf16[1,384,96]{1,2,0:T(8,128)(2,1)} %param.15) | copy-start | bytes 221188
  4.8 8.7 %collective-permute-start = (bf16[96,512]{1,0:T(8,128)(2,1)S(1)}, bf16[96,512]{1,0:T(8,128)(2,1)S(1)}, u32[]{:S(2)}, u32[]{:S(2)}) collective-permute-start(bf16[96,512]{1,0:T(8,128)(2,1)S(1)} %get-tuple-element.15), channel_id=1, source_target_pairs={{0,3},{1,2},{2,1},{3,0},{4,7},{5,6},{6,5},{7,4},{8,11},{9,10},{10,... | collective-permute-start | bytes 294920 | tf_op jit(solution)/shard_map/ppermute | solution.py:209
  8.8 6.0 %collective-permute-start.1 = (bf16[96,512]{1,0:T(8,128)(2,1)S(1)}, bf16[96,512]{1,0:T(8,128)(2,1)S(1)}, u32[]{:S(2)}, u32[]{:S(2)}) collective-permute-start(bf16[96,512]{1,0:T(8,128)(2,1)S(1)} %get-tuple-element.16), channel_id=1, source_target_pairs={{0,2},{1,3},{2,0},{3,1},{4,6},{5,7},{6,4},{7,5},{8,10},{9,11},{10,... | collective-permute-start | bytes 294920 | tf_op jit(solution)/shard_map/ppermute | solution.py:209
  9.3 6.2 %collective-permute-start.2 = (bf16[96,512]{1,0:T(8,128)(2,1)S(1)}, bf16[96,512]{1,0:T(8,128)(2,1)S(1)}, u32[]{:S(2)}, u32[]{:S(2)}) collective-permute-start(bf16[96,512]{1,0:T(8,128)(2,1)S(1)} %get-tuple-element.17), channel_id=1, source_target_pairs={{0,1},{1,0},{2,3},{3,2},{4,5},{5,4},{6,7},{7,6},{8,9},{9,8},{10,11... | collective-permute-start | bytes 294920 | tf_op jit(solution)/shard_map/ppermute | solution.py:209
  9.5 8.9 %collective-permute-start.3 = (bf16[96,512]{1,0:T(8,128)(2,1)S(1)}, bf16[96,512]{1,0:T(8,128)(2,1)S(1)}, u32[]{:S(2)}, u32[]{:S(2)}) collective-permute-start(bf16[96,512]{1,0:T(8,128)(2,1)S(1)} %get-tuple-element.20), channel_id=1, source_target_pairs={{0,3},{1,2},{2,1},{3,0},{4,7},{5,6},{6,5},{7,4},{8,11},{9,10},{10,... | collective-permute-start | bytes 294920 | tf_op jit(solution)/shard_map/ppermute | solution.py:209
  12.3 6.9 %collective-permute-start.4 = (bf16[96,512]{1,0:T(8,128)(2,1)S(1)}, bf16[96,512]{1,0:T(8,128)(2,1)S(1)}, u32[]{:S(2)}, u32[]{:S(2)}) collective-permute-start(bf16[96,512]{1,0:T(8,128)(2,1)S(1)} %get-tuple-element.21), channel_id=1, source_target_pairs={{0,2},{1,3},{2,0},{3,1},{4,6},{5,7},{6,4},{7,5},{8,10},{9,11},{10,... | collective-permute-start | bytes 294920 | tf_op jit(solution)/shard_map/ppermute | solution.py:209
  13.5 5.8 %collective-permute-start.5 = (bf16[96,512]{1,0:T(8,128)(2,1)S(1)}, bf16[96,512]{1,0:T(8,128)(2,1)S(1)}, u32[]{:S(2)}, u32[]{:S(2)}) collective-permute-start(bf16[96,512]{1,0:T(8,128)(2,1)S(1)} %get-tuple-element.22), channel_id=1, source_target_pairs={{0,1},{1,0},{2,3},{3,2},{4,5},{5,4},{6,7},{7,6},{8,9},{9,8},{10,11... | collective-permute-start | bytes 294920 | tf_op jit(solution)/shard_map/ppermute | solution.py:209
  15.5 6.3 %collective-permute-start.6 = (bf16[96,512]{1,0:T(8,128)(2,1)S(1)}, bf16[96,512]{1,0:T(8,128)(2,1)S(1)}, u32[]{:S(2)}, u32[]{:S(2)}) collective-permute-start(bf16[96,512]{1,0:T(8,128)(2,1)S(1)} %add_convert_fusion.1), channel_id=1, source_target_pairs={{0,4},{1,5},{2,6},{3,7},{4,0},{5,1},{6,2},{7,3},{8,12},{9,13},{10,... | collective-permute-start | bytes 294920 | tf_op jit(solution)/shard_map/ppermute | solution.py:209
  21.9 7.3 %collective-permute-start.7 = (bf16[96,896]{1,0:T(8,128)(2,1)S(1)}, bf16[96,896]{1,0:T(8,128)(2,1)S(1)}, u32[]{:S(2)}, u32[]{:S(2)}) collective-permute-start(bf16[96,896]{1,0:T(8,128)(2,1)S(1)} %pad_maximum_fusion), channel_id=1, source_target_pairs={{1,0},{2,1},{3,2},{4,3},{5,4},{6,5},{7,6},{9,8},{10,9},{11,10},{12... | collective-permute-start | bytes 516104 | tf_op jit(solution)/shard_map/ppermute | solution.py:212

commit v6 on v5

--- a/solution.py
+++ b/solution.py
@@ -10,6 +10,7 @@
 CROSS = 128
 CHUNKS = 4
 LANES = 128
+SPARE = 8
 F32 = jnp.float32
 BF16 = jnp.bfloat16
 NT = (((1,), (1,)), ((), ()))
@@ -61,7 +62,7 @@
     chunks = sems.shape[0]
     step = raw.shape[0] // chunks
     pieces = raw.shape[1] // LANES
-    att = picks.shape[0] // (len(slots) * pieces)
+    att = attach.shape[1]
 
     def fetch(i):
         rows = pl.ds(pl.multiple_of(i * step, step), step)
@@ -191,8 +192,8 @@
             pltpu.VMEM(damping.shape, F32),
             pltpu.VMEM(load_t.shape, F32),
             pltpu.VMEM((iface, modes), BF16),
-            pltpu.VMEM((iface * pieces, LANES), F32),
-            pltpu.VMEM((count * att * pieces, LANES), F32),
+            pltpu.VMEM((iface * pieces + SPARE, LANES), F32),
+            pltpu.VMEM((count * att * pieces + SPARE, LANES), F32),
             pltpu.VMEM((columns, modes), BF16),
             pltpu.SemaphoreType.DMA((chunks,)),
             pltpu.SemaphoreType.DMA((5,)),

time: 30.7 us -> 30.6 us (level)
  no operation moved by 1% of the time
where the time goes in v6:
time: 30.6 us; the launch traced here: 30.5 us
  starting transfers between devices  12.9 us (42%)
  waiting for transfers between devices  8.58 us (28%)
  Pallas kernels  7.42 us (24%)
  between operations  1.37 us (4%)
    ppermute x7, starting transfers between devices, swapped(): return lax.ppermute(value, 'mode', [(i, i ^ k) for i in range(count)])  11.6 us
    ppermute x7, waiting for transfers between devices, swapped(): return lax.ppermute(value, 'mode', [(i, i ^ k) for i in range(count)])  4.6 us
    pallas_call x1, Pallas kernels, per_device(): pl.pallas_call(functools.partial(parts_kernel, slots), out_shape=([part]...  4.1 us
    ppermute x1, waiting for transfers between devices, following(): return lax.ppermute(value, 'mode', [(i, i - 1) for i in range(1, count)])  3.98 us
    pallas_call x1, Pallas kernels, per_device(): pl.pallas_call(auto_kernel, out_shape=[jax.ShapeDtypeStruct((1, lines, 2,...  2.01 us
    pallas_call x1, Pallas kernels, per_device(): pl.pallas_call(joint_kernel, out_shape=jax.ShapeDtypeStruct((1, lines, 2,...  1.31 us
    ppermute x1, starting transfers between devices, following(): return lax.ppermute(value, 'mode', [(i, i - 1) for i in range(1, count)])  1.29 us
  transfers between devices with their start and end apart: 8, of which 5 were waited for; matrix products, arithmetic and copies ran while one was open for 0% of the time, Pallas kernels for 7%

profile of v6, /device:TPU:0, one launch (start us, length us, event | category | flops | bytes accessed | tf_op | source)
XLA Modules:
  0.0 30.5 jit_solution(13669814892466124931)
XLA Ops:
  0.6 0.0 copy-start
  0.6 4.1 %partial_sums.1 = (bf16[96,512]{1,0:T(8,128)(2,1)S(1)}, bf16[96,512]{1,0:T(8,128)(2,1)S(1)}, bf16[96,512]{1,0:T(8,128)(2,1)S(1)}, f32[96,512]{1,0:T(8,128)S(1)},...) custom-call(s32[8,96]{1,0:T(8,128)} %attach_hbm.1, ...), custom_call_target="tpu_custom_call" | custom-call | tf_op jit(solution)/shard_map/partial_sums/pallas_call | solution.py:183
  4.7 4.1 %collective-permute-start = (bf16[96,512]{1,0:T(8,128)(2,1)S(1)}, bf16[96,512]{1,0:T(8,128)(2,1)S(1)}, u32[]{:S(2)}, u32[]{:S(2)}) collective-permute-start(bf16[96,512]{1,0:T(8,128)(2,1)S(1)} %get-tuple-element.15), channel_id=1, source_target_pairs={{0,3},{1,2},{2,1},{3,0},{4,7},{5,6},{6,5},{7,4},{8,11},{9,10},{10,... | collective-permute-start | bytes 294920 | tf_op jit(solution)/shard_map/ppermute | solution.py:210
  8.8 0.4 %collective-permute-start.1 = (bf16[96,512]{1,0:T(8,128)(2,1)S(1)}, bf16[96,512]{1,0:T(8,128)(2,1)S(1)}, u32[]{:S(2)}, u32[]{:S(2)}) collective-permute-start(bf16[96,512]{1,0:T(8,128)(2,1)S(1)} %get-tuple-element.16), channel_id=1, source_target_pairs={{0,2},{1,3},{2,0},{3,1},{4,6},{5,7},{6,4},{7,5},{8,10},{9,11},{10,... | collective-permute-start | bytes 294920 | tf_op jit(solution)/shard_map/ppermute | solution.py:210
  9.2 0.2 collective-permute-start.2
  9.4 2.8 %collective-permute-start.3 = (bf16[96,512]{1,0:T(8,128)(2,1)S(1)}, bf16[96,512]{1,0:T(8,128)(2,1)S(1)}, u32[]{:S(2)}, u32[]{:S(2)}) collective-permute-start(bf16[96,512]{1,0:T(8,128)(2,1)S(1)} %get-tuple-element.20), channel_id=1, source_target_pairs={{0,3},{1,2},{2,1},{3,0},{4,7},{5,6},{6,5},{7,4},{8,11},{9,10},{10,... | collective-permute-start | bytes 294920 | tf_op jit(solution)/shard_map/ppermute | solution.py:210
  12.3 0.4 %collective-permute-start.4 = (bf16[96,512]{1,0:T(8,128)(2,1)S(1)}, bf16[96,512]{1,0:T(8,128)(2,1)S(1)}, u32[]{:S(2)}, u32[]{:S(2)}) collective-permute-start(bf16[96,512]{1,0:T(8,128)(2,1)S(1)} %get-tuple-element.21), channel_id=1, source_target_pairs={{0,2},{1,3},{2,0},{3,1},{4,6},{5,7},{6,4},{7,5},{8,10},{9,11},{10,... | collective-permute-start | bytes 294920 | tf_op jit(solution)/shard_map/ppermute | solution.py:210
  13.4 0.0 copy-done
  13.4 0.0 collective-permute-done
  13.4 0.7 %collective-permute-start.5 = (bf16[96,512]{1,0:T(8,128)(2,1)S(1)}, bf16[96,512]{1,0:T(8,128)(2,1)S(1)}, u32[]{:S(2)}, u32[]{:S(2)}) collective-permute-start(bf16[96,512]{1,0:T(8,128)(2,1)S(1)} %get-tuple-element.22), channel_id=1, source_target_pairs={{0,1},{1,0},{2,3},{3,2},{4,5},{5,4},{6,7},{7,6},{8,9},{9,8},{10,11... | collective-permute-start | bytes 294920 | tf_op jit(solution)/shard_map/ppermute | solution.py:210
  14.2 0.6 %collective-permute-done.1 = bf16[96,512]{1,0:T(8,128)(2,1)S(1)} collective-permute-done((bf16[96,512]{1,0:T(8,128)(2,1)S(1)}, bf16[96,512]{1,0:T(8,128)(2,1)S(1)}, u32[]{:S(2)}, u32[]{:S(2)}) %collective-permute-start.1) | collective-permute-done | bytes 98336 | tf_op jit(solution)/shard_map/ppermute | solution.py:210
  14.8 0.6 %collective-permute-done.2 = bf16[96,512]{1,0:T(8,128)(2,1)S(1)} collective-permute-done((bf16[96,512]{1,0:T(8,128)(2,1)S(1)}, bf16[96,512]{1,0:T(8,128)(2,1)S(1)}, u32[]{:S(2)}, u32[]{:S(2)}) %collective-permute-start.2) | collective-permute-done | bytes 98336 | tf_op jit(solution)/shard_map/ppermute | solution.py:210
  15.4 0.1 add_convert_fusion.1
  15.5 2.9 %collective-permute-start.6 = (bf16[96,512]{1,0:T(8,128)(2,1)S(1)}, bf16[96,512]{1,0:T(8,128)(2,1)S(1)}, u32[]{:S(2)}, u32[]{:S(2)}) collective-permute-start(bf16[96,512]{1,0:T(8,128)(2,1)S(1)} %add_convert_fusion.1), channel_id=1, source_target_pairs={{0,4},{1,5},{2,6},{3,7},{4,0},{5,1},{6,2},{7,3},{8,12},{9,13},{10,... | collective-permute-start | bytes 294920 | tf_op jit(solution)/shard_map/ppermute | solution.py:210
  18.4 0.0 collective-permute-done.3
  18.4 0.8 %collective-permute-done.4 = bf16[96,512]{1,0:T(8,128)(2,1)S(1)} collective-permute-done((bf16[96,512]{1,0:T(8,128)(2,1)S(1)}, bf16[96,512]{1,0:T(8,128)(2,1)S(1)}, u32[]{:S(2)}, u32[]{:S(2)}) %collective-permute-start.4) | collective-permute-done | bytes 98336 | tf_op jit(solution)/shard_map/ppermute | solution.py:210
  19.2 0.0 collective-permute-done.5
  19.2 2.5 %collective-permute-done.6 = bf16[96,512]{1,0:T(8,128)(2,1)S(1)} collective-permute-done((bf16[96,512]{1,0:T(8,128)(2,1)S(1)}, bf16[96,512]{1,0:T(8,128)(2,1)S(1)}, u32[]{:S(2)}, u32[]{:S(2)}) %collective-permute-start.6) | collective-permute-done | bytes 98336 | tf_op jit(solution)/shard_map/ppermute | solution.py:210
  21.7 0.1 add_convert_fusion.picked_ref
  21.8 1.3 %collective-permute-start.7 = (bf16[96,896]{1,0:T(8,128)(2,1)S(1)}, bf16[96,896]{1,0:T(8,128)(2,1)S(1)}, u32[]{:S(2)}, u32[]{:S(2)}) collective-permute-start(bf16[96,896]{1,0:T(8,128)(2,1)S(1)} %pad_maximum_fusion), channel_id=1, source_target_pairs={{1,0},{2,1},{3,2},{4,3},{5,4},{6,5},{7,6},{9,8},{10,9},{11,10},{12... | collective-permute-start | bytes 516104 | tf_op jit(solution)/shard_map/ppermute | solution.py:213
  23.1 2.0 %auto_csd.1 = (bf16[1,4,2,384,384]{4,3,2,1,0:T(8,128)(2,1)}, bf16[256,512]{1,0:T(8,128)(2,1)S(1)}) custom-call(bf16[96,384]{1,0:T(8,128)(2,1)S(1)} %fusion.otm_ref, bf16[96,512]{1,0:T(8,128)(2,1)S(1)} %add_convert_fusion.picked_ref), custom_call_target="tpu_custom_call" | custom-call | tf_op jit(solution)/shard_map/auto_csd/pallas_call | solution.py:227
  25.2 4.0 %collective-permute-done.7.joined_ref = bf16[96,896]{1,0:T(8,128)(2,1)S(1)} collective-permute-done((bf16[96,896]{1,0:T(8,128)(2,1)S(1)}, bf16[96,896]{1,0:T(8,128)(2,1)S(1)}, u32[]{:S(2)}, u32[]{:S(2)}) %collective-permute-start.7) | collective-permute-done | bytes 172064 | tf_op jit(solution)/shard_map/ppermute | solution.py:213
  29.1 1.3 %joint_csd.1 = bf16[1,4,2,128,384]{4,3,2,1,0:T(8,128)(2,1)} custom-call(bf16[256,512]{1,0:T(8,128)(2,1)S(1)} %get-tuple-element.25.left_ref, bf16[96,896]{1,0:T(8,128)(2,1)S(1)} %collective-permute-done.7.joined_ref), custom_call_target="tpu_custom_call" | custom-call | tf_op jit(solution)/shard_map/joint_csd/pallas_call | solution.py:242
  (3 shorter events, 0.0 us)
Async XLA Ops:
  0.6 12.8 %copy-start = (bf16[1,384,96]{1,2,0:T(8,128)(2,1)S(1)}, bf16[1,384,96]{1,2,0:T(8,128)(2,1)}, u32[]{:S(2)}) copy-start(bf16[1,384,96]{1,2,0:T(8,128)(2,1)} %param.15) | copy-start | bytes 221188
  4.7 8.7 %collective-permute-start = (bf16[96,512]{1,0:T(8,128)(2,1)S(1)}, bf16[96,512]{1,0:T(8,128)(2,1)S(1)}, u32[]{:S(2)}, u32[]{:S(2)}) collective-permute-start(bf16[96,512]{1,0:T(8,128)(2,1)S(1)} %get-tuple-element.15), channel_id=1, source_target_pairs={{0,3},{1,2},{2,1},{3,0},{4,7},{5,6},{6,5},{7,4},{8,11},{9,10},{10,... | collective-permute-start | bytes 294920 | tf_op jit(solution)/shard_map/ppermute | solution.py:210
  8.8 6.0 %collective-permute-start.1 = (bf16[96,512]{1,0:T(8,128)(2,1)S(1)}, bf16[96,512]{1,0:T(8,128)(2,1)S(1)}, u32[]{:S(2)}, u32[]{:S(2)}) collective-permute-start(bf16[96,512]{1,0:T(8,128)(2,1)S(1)} %get-tuple-element.16), channel_id=1, source_target_pairs={{0,2},{1,3},{2,0},{3,1},{4,6},{5,7},{6,4},{7,5},{8,10},{9,11},{10,... | collective-permute-start | bytes 294920 | tf_op jit(solution)/shard_map/ppermute | solution.py:210
  9.2 6.2 %collective-permute-start.2 = (bf16[96,512]{1,0:T(8,128)(2,1)S(1)}, bf16[96,512]{1,0:T(8,128)(2,1)S(1)}, u32[]{:S(2)}, u32[]{:S(2)}) collective-permute-start(bf16[96,512]{1,0:T(8,128)(2,1)S(1)} %get-tuple-element.17), channel_id=1, source_target_pairs={{0,1},{1,0},{2,3},{3,2},{4,5},{5,4},{6,7},{7,6},{8,9},{9,8},{10,11... | collective-permute-start | bytes 294920 | tf_op jit(solution)/shard_map/ppermute | solution.py:210
  9.4 8.9 %collective-permute-start.3 = (bf16[96,512]{1,0:T(8,128)(2,1)S(1)}, bf16[96,512]{1,0:T(8,128)(2,1)S(1)}, u32[]{:S(2)}, u32[]{:S(2)}) collective-permute-start(bf16[96,512]{1,0:T(8,128)(2,1)S(1)} %get-tuple-element.20), channel_id=1, source_target_pairs={{0,3},{1,2},{2,1},{3,0},{4,7},{5,6},{6,5},{7,4},{8,11},{9,10},{10,... | collective-permute-start | bytes 294920 | tf_op jit(solution)/shard_map/ppermute | solution.py:210
  12.3 6.9 %collective-permute-start.4 = (bf16[96,512]{1,0:T(8,128)(2,1)S(1)}, bf16[96,512]{1,0:T(8,128)(2,1)S(1)}, u32[]{:S(2)}, u32[]{:S(2)}) collective-permute-start(bf16[96,512]{1,0:T(8,128)(2,1)S(1)} %get-tuple-element.21), channel_id=1, source_target_pairs={{0,2},{1,3},{2,0},{3,1},{4,6},{5,7},{6,4},{7,5},{8,10},{9,11},{10,... | collective-permute-start | bytes 294920 | tf_op jit(solution)/shard_map/ppermute | solution.py:210
  13.4 5.8 %collective-permute-start.5 = (bf16[96,512]{1,0:T(8,128)(2,1)S(1)}, bf16[96,512]{1,0:T(8,128)(2,1)S(1)}, u32[]{:S(2)}, u32[]{:S(2)}) collective-permute-start(bf16[96,512]{1,0:T(8,128)(2,1)S(1)} %get-tuple-element.22), channel_id=1, source_target_pairs={{0,1},{1,0},{2,3},{3,2},{4,5},{5,4},{6,7},{7,6},{8,9},{9,8},{10,11... | collective-permute-start | bytes 294920 | tf_op jit(solution)/shard_map/ppermute | solution.py:210
  15.5 6.3 %collective-permute-start.6 = (bf16[96,512]{1,0:T(8,128)(2,1)S(1)}, bf16[96,512]{1,0:T(8,128)(2,1)S(1)}, u32[]{:S(2)}, u32[]{:S(2)}) collective-permute-start(bf16[96,512]{1,0:T(8,128)(2,1)S(1)} %add_convert_fusion.1), channel_id=1, source_target_pairs={{0,4},{1,5},{2,6},{3,7},{4,0},{5,1},{6,2},{7,3},{8,12},{9,13},{10,... | collective-permute-start | bytes 294920 | tf_op jit(solution)/shard_map/ppermute | solution.py:210
  21.8 7.3 %collective-permute-start.7 = (bf16[96,896]{1,0:T(8,128)(2,1)S(1)}, bf16[96,896]{1,0:T(8,128)(2,1)S(1)}, u32[]{:S(2)}, u32[]{:S(2)}) collective-permute-start(bf16[96,896]{1,0:T(8,128)(2,1)S(1)} %pad_maximum_fusion), channel_id=1, source_target_pairs={{1,0},{2,1},{3,2},{4,3},{5,4},{6,5},{7,6},{9,8},{10,9},{11,10},{12... | collective-permute-start | bytes 516104 | tf_op jit(solution)/shard_map/ppermute | solution.py:213

commit v7 on v6

--- a/solution.py
+++ b/solution.py
@@ -8,7 +8,7 @@
 from jax.sharding import PartitionSpec as P
 
 CROSS = 128
-CHUNKS = 4
+CHUNKS = 6
 LANES = 128
 SPARE = 8
 F32 = jnp.float32

time: 30.6 us -> 30.6 us (level)
  no operation moved by 1% of the time
where the time goes in v7:
time: 30.6 us; the launch traced here: 30.4 us
  starting transfers between devices  12.9 us (42%)
  waiting for transfers between devices  8.56 us (28%)
  Pallas kernels  7.37 us (24%)
  between operations  1.37 us (4%)
    ppermute x7, starting transfers between devices, swapped(): return lax.ppermute(value, 'mode', [(i, i ^ k) for i in range(count)])  11.6 us
    ppermute x7, waiting for transfers between devices, swapped(): return lax.ppermute(value, 'mode', [(i, i ^ k) for i in range(count)])  4.58 us
    pallas_call x1, Pallas kernels, per_device(): pl.pallas_call(functools.partial(parts_kernel, slots), out_shape=([part]...  4.05 us
    ppermute x1, waiting for transfers between devices, following(): return lax.ppermute(value, 'mode', [(i, i - 1) for i in range(1, count)])  3.98 us
    pallas_call x1, Pallas kernels, per_device(): pl.pallas_call(auto_kernel, out_shape=[jax.ShapeDtypeStruct((1, lines, 2,...  2.02 us
    pallas_call x1, Pallas kernels, per_device(): pl.pallas_call(joint_kernel, out_shape=jax.ShapeDtypeStruct((1, lines, 2,...  1.31 us
    ppermute x1, starting transfers between devices, following(): return lax.ppermute(value, 'mode', [(i, i - 1) for i in range(1, count)])  1.29 us
  transfers between devices with their start and end apart: 8, of which 5 were waited for; matrix products, arithmetic and copies ran while one was open for 0% of the time, Pallas kernels for 7%

profile of v7, /device:TPU:0, one launch (start us, length us, event | category | flops | bytes accessed | tf_op | source)
XLA Modules:
  0.0 30.4 jit_solution(8022338730223833163)
XLA Ops:
  0.6 0.0 copy-start
  0.6 4.0 %partial_sums.1 = (bf16[96,512]{1,0:T(8,128)(2,1)S(1)}, bf16[96,512]{1,0:T(8,128)(2,1)S(1)}, bf16[96,512]{1,0:T(8,128)(2,1)S(1)}, f32[96,512]{1,0:T(8,128)S(1)},...) custom-call(s32[8,96]{1,0:T(8,128)} %attach_hbm.1, ...), custom_call_target="tpu_custom_call" | custom-call | tf_op jit(solution)/shard_map/partial_sums/pallas_call | solution.py:183
  4.7 4.1 %collective-permute-start = (bf16[96,512]{1,0:T(8,128)(2,1)S(1)}, bf16[96,512]{1,0:T(8,128)(2,1)S(1)}, u32[]{:S(2)}, u32[]{:S(2)}) collective-permute-start(bf16[96,512]{1,0:T(8,128)(2,1)S(1)} %get-tuple-element.15), channel_id=1, source_target_pairs={{0,3},{1,2},{2,1},{3,0},{4,7},{5,6},{6,5},{7,4},{8,11},{9,10},{10,... | collective-permute-start | bytes 294920 | tf_op jit(solution)/shard_map/ppermute | solution.py:210
  8.8 0.4 %collective-permute-start.1 = (bf16[96,512]{1,0:T(8,128)(2,1)S(1)}, bf16[96,512]{1,0:T(8,128)(2,1)S(1)}, u32[]{:S(2)}, u32[]{:S(2)}) collective-permute-start(bf16[96,512]{1,0:T(8,128)(2,1)S(1)} %get-tuple-element.16), channel_id=1, source_target_pairs={{0,2},{1,3},{2,0},{3,1},{4,6},{5,7},{6,4},{7,5},{8,10},{9,11},{10,... | collective-permute-start | bytes 294920 | tf_op jit(solution)/shard_map/ppermute | solution.py:210
  9.2 0.2 collective-permute-start.2
  9.4 2.8 %collective-permute-start.3 = (bf16[96,512]{1,0:T(8,128)(2,1)S(1)}, bf16[96,512]{1,0:T(8,128)(2,1)S(1)}, u32[]{:S(2)}, u32[]{:S(2)}) collective-permute-start(bf16[96,512]{1,0:T(8,128)(2,1)S(1)} %get-tuple-element.20), channel_id=1, source_target_pairs={{0,3},{1,2},{2,1},{3,0},{4,7},{5,6},{6,5},{7,4},{8,11},{9,10},{10,... | collective-permute-start | bytes 294920 | tf_op jit(solution)/shard_map/ppermute | solution.py:210
  12.2 0.4 %collective-permute-start.4 = (bf16[96,512]{1,0:T(8,128)(2,1)S(1)}, bf16[96,512]{1,0:T(8,128)(2,1)S(1)}, u32[]{:S(2)}, u32[]{:S(2)}) collective-permute-start(bf16[96,512]{1,0:T(8,128)(2,1)S(1)} %get-tuple-element.21), channel_id=1, source_target_pairs={{0,2},{1,3},{2,0},{3,1},{4,6},{5,7},{6,4},{7,5},{8,10},{9,11},{10,... | collective-permute-start | bytes 294920 | tf_op jit(solution)/shard_map/ppermute | solution.py:210
  13.3 0.0 copy-done
  13.4 0.0 collective-permute-done
  13.4 0.7 %collective-permute-start.5 = (bf16[96,512]{1,0:T(8,128)(2,1)S(1)}, bf16[96,512]{1,0:T(8,128)(2,1)S(1)}, u32[]{:S(2)}, u32[]{:S(2)}) collective-permute-start(bf16[96,512]{1,0:T(8,128)(2,1)S(1)} %get-tuple-element.22), channel_id=1, source_target_pairs={{0,1},{1,0},{2,3},{3,2},{4,5},{5,4},{6,7},{7,6},{8,9},{9,8},{10,11... | collective-permute-start | bytes 294920 | tf_op jit(solution)/shard_map/ppermute | solution.py:210
  14.1 0.6 %collective-permute-done.1 = bf16[96,512]{1,0:T(8,128)(2,1)S(1)} collective-permute-done((bf16[96,512]{1,0:T(8,128)(2,1)S(1)}, bf16[96,512]{1,0:T(8,128)(2,1)S(1)}, u32[]{:S(2)}, u32[]{:S(2)}) %collective-permute-start.1) | collective-permute-done | bytes 98336 | tf_op jit(solution)/shard_map/ppermute | solution.py:210
  14.8 0.6 %collective-permute-done.2 = bf16[96,512]{1,0:T(8,128)(2,1)S(1)} collective-permute-done((bf16[96,512]{1,0:T(8,128)(2,1)S(1)}, bf16[96,512]{1,0:T(8,128)(2,1)S(1)}, u32[]{:S(2)}, u32[]{:S(2)}) %collective-permute-start.2) | collective-permute-done | bytes 98336 | tf_op jit(solution)/shard_map/ppermute | solution.py:210
  15.3 0.1 add_convert_fusion.1
  15.4 2.9 %collective-permute-start.6 = (bf16[96,512]{1,0:T(8,128)(2,1)S(1)}, bf16[96,512]{1,0:T(8,128)(2,1)S(1)}, u32[]{:S(2)}, u32[]{:S(2)}) collective-permute-start(bf16[96,512]{1,0:T(8,128)(2,1)S(1)} %add_convert_fusion.1), channel_id=1, source_target_pairs={{0,4},{1,5},{2,6},{3,7},{4,0},{5,1},{6,2},{7,3},{8,12},{9,13},{10,... | collective-permute-start | bytes 294920 | tf_op jit(solution)/shard_map/ppermute | solution.py:210
  18.3 0.0 collective-permute-done.3
  18.3 0.8 %collective-permute-done.4 = bf16[96,512]{1,0:T(8,128)(2,1)S(1)} collective-permute-done((bf16[96,512]{1,0:T(8,128)(2,1)S(1)}, bf16[96,512]{1,0:T(8,128)(2,1)S(1)}, u32[]{:S(2)}, u32[]{:S(2)}) %collective-permute-start.4) | collective-permute-done | bytes 98336 | tf_op jit(solution)/shard_map/ppermute | solution.py:210
  19.2 0.0 collective-permute-done.5
  19.2 2.5 %collective-permute-done.6 = bf16[96,512]{1,0:T(8,128)(2,1)S(1)} collective-permute-done((bf16[96,512]{1,0:T(8,128)(2,1)S(1)}, bf16[96,512]{1,0:T(8,128)(2,1)S(1)}, u32[]{:S(2)}, u32[]{:S(2)}) %collective-permute-start.6) | collective-permute-done | bytes 98336 | tf_op jit(solution)/shard_map/ppermute | solution.py:210
  21.7 0.1 add_convert_fusion.picked_ref
  21.8 1.3 %collective-permute-start.7 = (bf16[96,896]{1,0:T(8,128)(2,1)S(1)}, bf16[96,896]{1,0:T(8,128)(2,1)S(1)}, u32[]{:S(2)}, u32[]{:S(2)}) collective-permute-start(bf16[96,896]{1,0:T(8,128)(2,1)S(1)} %pad_maximum_fusion), channel_id=1, source_target_pairs={{1,0},{2,1},{3,2},{4,3},{5,4},{6,5},{7,6},{9,8},{10,9},{11,10},{12... | collective-permute-start | bytes 516104 | tf_op jit(solution)/shard_map/ppermute | solution.py:213
  23.1 2.0 %auto_csd.1 = (bf16[1,4,2,384,384]{4,3,2,1,0:T(8,128)(2,1)}, bf16[256,512]{1,0:T(8,128)(2,1)S(1)}) custom-call(bf16[96,384]{1,0:T(8,128)(2,1)S(1)} %fusion.otm_ref, bf16[96,512]{1,0:T(8,128)(2,1)S(1)} %add_convert_fusion.picked_ref), custom_call_target="tpu_custom_call" | custom-call | tf_op jit(solution)/shard_map/auto_csd/pallas_call | solution.py:227
  25.1 4.0 %collective-permute-done.7.joined_ref = bf16[96,896]{1,0:T(8,128)(2,1)S(1)} collective-permute-done((bf16[96,896]{1,0:T(8,128)(2,1)S(1)}, bf16[96,896]{1,0:T(8,128)(2,1)S(1)}, u32[]{:S(2)}, u32[]{:S(2)}) %collective-permute-start.7) | collective-permute-done | bytes 172064 | tf_op jit(solution)/shard_map/ppermute | solution.py:213
  29.1 1.3 %joint_csd.1 = bf16[1,4,2,128,384]{4,3,2,1,0:T(8,128)(2,1)} custom-call(bf16[256,512]{1,0:T(8,128)(2,1)S(1)} %get-tuple-element.25.left_ref, bf16[96,896]{1,0:T(8,128)(2,1)S(1)} %collective-permute-done.7.joined_ref), custom_call_target="tpu_custom_call" | custom-call | tf_op jit(solution)/shard_map/joint_csd/pallas_call | solution.py:242
  (3 shorter events, 0.0 us)
Async XLA Ops:
  0.6 12.7 %copy-start = (bf16[1,384,96]{1,2,0:T(8,128)(2,1)S(1)}, bf16[1,384,96]{1,2,0:T(8,128)(2,1)}, u32[]{:S(2)}) copy-start(bf16[1,384,96]{1,2,0:T(8,128)(2,1)} %param.15) | copy-start | bytes 221188
  4.7 8.7 %collective-permute-start = (bf16[96,512]{1,0:T(8,128)(2,1)S(1)}, bf16[96,512]{1,0:T(8,128)(2,1)S(1)}, u32[]{:S(2)}, u32[]{:S(2)}) collective-permute-start(bf16[96,512]{1,0:T(8,128)(2,1)S(1)} %get-tuple-element.15), channel_id=1, source_target_pairs={{0,3},{1,2},{2,1},{3,0},{4,7},{5,6},{6,5},{7,4},{8,11},{9,10},{10,... | collective-permute-start | bytes 294920 | tf_op jit(solution)/shard_map/ppermute | solution.py:210
  8.8 6.0 %collective-permute-start.1 = (bf16[96,512]{1,0:T(8,128)(2,1)S(1)}, bf16[96,512]{1,0:T(8,128)(2,1)S(1)}, u32[]{:S(2)}, u32[]{:S(2)}) collective-permute-start(bf16[96,512]{1,0:T(8,128)(2,1)S(1)} %get-tuple-element.16), channel_id=1, source_target_pairs={{0,2},{1,3},{2,0},{3,1},{4,6},{5,7},{6,4},{7,5},{8,10},{9,11},{10,... | collective-permute-start | bytes 294920 | tf_op jit(solution)/shard_map/ppermute | solution.py:210
  9.2 6.2 %collective-permute-start.2 = (bf16[96,512]{1,0:T(8,128)(2,1)S(1)}, bf16[96,512]{1,0:T(8,128)(2,1)S(1)}, u32[]{:S(2)}, u32[]{:S(2)}) collective-permute-start(bf16[96,512]{1,0:T(8,128)(2,1)S(1)} %get-tuple-element.17), channel_id=1, source_target_pairs={{0,1},{1,0},{2,3},{3,2},{4,5},{5,4},{6,7},{7,6},{8,9},{9,8},{10,11... | collective-permute-start | bytes 294920 | tf_op jit(solution)/shard_map/ppermute | solution.py:210
  9.4 8.9 %collective-permute-start.3 = (bf16[96,512]{1,0:T(8,128)(2,1)S(1)}, bf16[96,512]{1,0:T(8,128)(2,1)S(1)}, u32[]{:S(2)}, u32[]{:S(2)}) collective-permute-start(bf16[96,512]{1,0:T(8,128)(2,1)S(1)} %get-tuple-element.20), channel_id=1, source_target_pairs={{0,3},{1,2},{2,1},{3,0},{4,7},{5,6},{6,5},{7,4},{8,11},{9,10},{10,... | collective-permute-start | bytes 294920 | tf_op jit(solution)/shard_map/ppermute | solution.py:210
  12.2 6.9 %collective-permute-start.4 = (bf16[96,512]{1,0:T(8,128)(2,1)S(1)}, bf16[96,512]{1,0:T(8,128)(2,1)S(1)}, u32[]{:S(2)}, u32[]{:S(2)}) collective-permute-start(bf16[96,512]{1,0:T(8,128)(2,1)S(1)} %get-tuple-element.21), channel_id=1, source_target_pairs={{0,2},{1,3},{2,0},{3,1},{4,6},{5,7},{6,4},{7,5},{8,10},{9,11},{10,... | collective-permute-start | bytes 294920 | tf_op jit(solution)/shard_map/ppermute | solution.py:210
  13.4 5.8 %collective-permute-start.5 = (bf16[96,512]{1,0:T(8,128)(2,1)S(1)}, bf16[96,512]{1,0:T(8,128)(2,1)S(1)}, u32[]{:S(2)}, u32[]{:S(2)}) collective-permute-start(bf16[96,512]{1,0:T(8,128)(2,1)S(1)} %get-tuple-element.22), channel_id=1, source_target_pairs={{0,1},{1,0},{2,3},{3,2},{4,5},{5,4},{6,7},{7,6},{8,9},{9,8},{10,11... | collective-permute-start | bytes 294920 | tf_op jit(solution)/shard_map/ppermute | solution.py:210
  15.4 6.3 %collective-permute-start.6 = (bf16[96,512]{1,0:T(8,128)(2,1)S(1)}, bf16[96,512]{1,0:T(8,128)(2,1)S(1)}, u32[]{:S(2)}, u32[]{:S(2)}) collective-permute-start(bf16[96,512]{1,0:T(8,128)(2,1)S(1)} %add_convert_fusion.1), channel_id=1, source_target_pairs={{0,4},{1,5},{2,6},{3,7},{4,0},{5,1},{6,2},{7,3},{8,12},{9,13},{10,... | collective-permute-start | bytes 294920 | tf_op jit(solution)/shard_map/ppermute | solution.py:210
  21.8 7.3 %collective-permute-start.7 = (bf16[96,896]{1,0:T(8,128)(2,1)S(1)}, bf16[96,896]{1,0:T(8,128)(2,1)S(1)}, u32[]{:S(2)}, u32[]{:S(2)}) collective-permute-start(bf16[96,896]{1,0:T(8,128)(2,1)S(1)} %pad_maximum_fusion), channel_id=1, source_target_pairs={{1,0},{2,1},{3,2},{4,3},{5,4},{6,5},{7,6},{9,8},{10,9},{11,10},{12... | collective-permute-start | bytes 516104 | tf_op jit(solution)/shard_map/ppermute | solution.py:213
